TPU v7x, 32 devices: a whole 2x2x4 slice. The times are simulated.
32 devices in a mesh: dp: 8 (over z, x), tensor: 4 (over y, core).
Axes of the slice: x: 2, y: 2, z: 4, core: 2. Of those that a mesh axis runs over, the one named last changes fastest.
Arguments:
- inputs: bfloat16 [8192, 2048], P(('dp', 'tensor')), may hold values from -6 to 6
- cotangent: bfloat16 [8192, 2048], P(('dp', 'tensor')), may hold values from -6 to 6
- qkv_weight: float32 [2048, 3, 2048], P('dp', None, 'tensor'), may hold values from -0.125 to 0.125
- qkv_first: float32 [2048, 3, 2048], P('dp', None, 'tensor'), may hold values from -64 to 64
- qkv_second: float32 [2048, 3, 2048], P('dp', None, 'tensor'), may hold values from 8.192 to 32.768
- dense_weight: float32 [2048, 2048], P('dp', 'tensor'), may hold values from -0.5 to 0.5
- dense_first: float32 [2048, 2048], P('dp', 'tensor'), may hold values from -4 to 4
- dense_second: float32 [2048, 2048], P('dp', 'tensor'), may hold values from 0.04 to 0.16
- up_weight: float32 [2048, 8192], P('dp', 'tensor'), may hold values from -0.125 to 0.125
- up_first: float32 [2048, 8192], P('dp', 'tensor'), may hold values from -16 to 16
- up_second: float32 [2048, 8192], P('dp', 'tensor'), may hold values from 0.73728 to 2.94912
- down_weight: float32 [2048, 8192], P('dp', 'tensor'), may hold values from -0.0625 to 0.0625
- down_first: float32 [2048, 8192], P('dp', 'tensor'), may hold values from -32 to 32
- down_second: float32 [2048, 8192], P('dp', 'tensor'), may hold values from 2.94912 to 11.79648
- qkv_bias: float32 [3, 2048], P(None, ('tensor', 'dp')), may hold values from -1.25 to 1.25
- qkv_bias_first: float32 [3, 2048], P(None, ('tensor', 'dp')), may hold values from -64 to 64
- qkv_bias_second: float32 [3, 2048], P(None, ('tensor', 'dp')), may hold values from 8.192 to 32.768
- up_bias: float32 [8192], P(('tensor', 'dp')), may hold values from -1.25 to 1.25
- up_bias_first: float32 [8192], P(('tensor', 'dp')), may hold values from -16 to 16
- up_bias_second: float32 [8192], P(('tensor', 'dp')), may hold values from 0.73728 to 2.94912
- norm_vectors: float32 [4, 2048], P(None, 'dp'), may hold values from -0.6 to 1.3, as said below
- norm_first: float32 [4, 2048], P(None, 'dp'), may hold values from -64 to 64
- norm_second: float32 [4, 2048], P(None, 'dp'), may hold values from 8.192 to 32.768
Outputs:
- output: bfloat16 [8192, 2048], P(('dp', 'tensor'))
- input_grad: float32 [8192, 2048], P(('dp', 'tensor'))
- qkv_grad: float32 [2048, 3, 2048], P('dp', None, 'tensor')
- qkv_new: float32 [2048, 3, 2048], P('dp', None, 'tensor')
- qkv_first_new: float32 [2048, 3, 2048], P('dp', None, 'tensor')
- qkv_second_new: float32 [2048, 3, 2048], P('dp', None, 'tensor')
- dense_grad: float32 [2048, 2048], P('dp', 'tensor')
- dense_new: float32 [2048, 2048], P('dp', 'tensor')
- dense_first_new: float32 [2048, 2048], P('dp', 'tensor')
- dense_second_new: float32 [2048, 2048], P('dp', 'tensor')
- up_grad: float32 [2048, 8192], P('dp', 'tensor')
- up_new: float32 [2048, 8192], P('dp', 'tensor')
- up_first_new: float32 [2048, 8192], P('dp', 'tensor')
- up_second_new: float32 [2048, 8192], P('dp', 'tensor')
- down_grad: float32 [2048, 8192], P('dp', 'tensor')
- down_new: float32 [2048, 8192], P('dp', 'tensor')
- down_first_new: float32 [2048, 8192], P('dp', 'tensor')
- down_second_new: float32 [2048, 8192], P('dp', 'tensor')
- qkv_bias_grad: float32 [3, 2048], P(None, ('tensor', 'dp'))
- qkv_bias_new: float32 [3, 2048], P(None, ('tensor', 'dp'))
- qkv_bias_first_new: float32 [3, 2048], P(None, ('tensor', 'dp'))
- qkv_bias_second_new: float32 [3, 2048], P(None, ('tensor', 'dp'))
- up_bias_grad: float32 [8192], P(('tensor', 'dp'))
- up_bias_new: float32 [8192], P(('tensor', 'dp'))
- up_bias_first_new: float32 [8192], P(('tensor', 'dp'))
- up_bias_second_new: float32 [8192], P(('tensor', 'dp'))
- norm_grad: float32 [4, 2048], P(None, 'dp')
- norm_new: float32 [4, 2048], P(None, 'dp')
- norm_first_new: float32 [4, 2048], P(None, 'dp')
- norm_second_new: float32 [4, 2048], P(None, 'dp')
Inputs may be any that keep to these rules, and one draw needn't show every extreme that they name: `norm_vectors`: row 0 lies near 1, rows 1 to 3 near 0.
All inputs are finite; a program needn't handle non-finite values.
Results may differ from a plain program's by a relative error of at most 0.012.
The roundings to bfloat16 on the way count: a program that leaves them out, or rounds other values in their place, can miss the bound.
Values may be sent and summed in bfloat16 or wider, within the bound.
A program may use at most 256 MiB of HBM per device.

v0:
```python
from functools import partial

import jax
import jax.numpy as jnp
from jax import lax
from jax.sharding import PartitionSpec as P

HEAD = 64
ROT = 32
LENGTH = 1024
STEP = 10


norm_eps = 1e-05
beta_one = 0.9
beta_two = 0.999
epsilon = 1e-08
masked = -1e30


def angles(positions):
    steps_half = jnp.arange(ROT // 2, dtype=jnp.float32)
    inverse = 1.0 / 10000.0 ** (steps_half * 2.0 / ROT)
    turned = positions[:, None] * inverse[None, :]
    return (jnp.cos(turned), jnp.sin(turned))


def rotate(field, cosine, sine):
    half = ROT // 2
    first = field[..., :half]
    second = field[..., half:ROT]
    cos_wide = cosine[:, None, :]
    sin_wide = sine[:, None, :]
    return jnp.concatenate(
        [
            first * cos_wide - second * sin_wide,
            second * cos_wide + first * sin_wide,
            field[..., ROT:],
        ],
        axis=-1,
    )


def rotate_back(field, cosine, sine):
    half = ROT // 2
    first = field[..., :half]
    second = field[..., half:ROT]
    cos_wide = cosine[:, None, :]
    sin_wide = sine[:, None, :]
    return jnp.concatenate(
        [
            first * cos_wide + second * sin_wide,
            second * cos_wide - first * sin_wide,
            field[..., ROT:],
        ],
        axis=-1,
    )


def score_block(part, keys, start):
    block = part.shape[0]
    scores = jnp.einsum("bhe,lhe->hbl", part, keys, preferred_element_type=jnp.float32) * HEAD ** (
        -0.5
    )
    place = start + jnp.arange(block, dtype=jnp.int32)
    allowed = jnp.arange(keys.shape[0], dtype=jnp.int32)[None, :] <= place[:, None]
    return jnp.where(allowed[None], scores, masked)


def attend_sequence(items):
    query, keys, values = items
    block = min(512, LENGTH)
    starts = jnp.arange(LENGTH // block, dtype=jnp.int32) * block

    def one_block(start):
        part = lax.dynamic_slice_in_dim(query, start, block, 0)
        scores = score_block(part, keys, start)
        top = jnp.max(scores, axis=2, keepdims=True)
        expo = jnp.exp(scores - top)
        total = jnp.sum(expo, axis=2, keepdims=True)
        probs = (expo / total).astype(jnp.bfloat16)
        mixed = jnp.einsum("hbl,lhe->bhe", probs, values, preferred_element_type=jnp.float32)
        return (mixed.astype(jnp.bfloat16), top, total)

    mixed, top, total = lax.map(one_block, starts)
    return (mixed.reshape(LENGTH, -1), top, total)


def attend_back(items):
    query, keys, values, grad_mixed, top, total = items
    block = min(512, LENGTH)
    starts = jnp.arange(LENGTH // block, dtype=jnp.int32) * block
    factor = HEAD ** (-0.5)

    def one_block(carry, pieces):
        grad_keys, grad_values = carry
        start, top_now, total_now = pieces
        part = lax.dynamic_slice_in_dim(query, start, block, 0)
        grad_part = lax.dynamic_slice_in_dim(grad_mixed, start, block, 0)
        scores = score_block(part, keys, start)
        probs = jnp.exp(scores - top_now) / total_now
        grad_probs = jnp.einsum(
            "bhe,lhe->hbl", grad_part, values, preferred_element_type=jnp.float32
        )
        inner = jnp.sum(probs * grad_probs, axis=2, keepdims=True)
        grad_scores = (probs * (grad_probs - inner)).astype(jnp.bfloat16)
        grad_query = (
            jnp.einsum("hbl,lhe->bhe", grad_scores, keys, preferred_element_type=jnp.float32)
            * factor
        )
        grad_keys = (
            grad_keys
            + jnp.einsum("hbl,bhe->lhe", grad_scores, part, preferred_element_type=jnp.float32)
            * factor
        )
        grad_values = grad_values + jnp.einsum(
            "hbl,bhe->lhe",
            probs.astype(jnp.bfloat16),
            grad_part,
            preferred_element_type=jnp.float32,
        )
        return ((grad_keys, grad_values), grad_query)

    zeros = jnp.zeros(keys.shape, jnp.float32)
    (grad_keys, grad_values), grad_query = lax.scan(one_block, (zeros, zeros), (starts, top, total))
    return (grad_query.reshape(keys.shape), grad_keys, grad_values)


def adam(weight, grad, first, second, rate, decay):
    first_new = beta_one * first + (1.0 - beta_one) * grad
    second_new = beta_two * second + (1.0 - beta_two) * grad * grad
    scaled_first = first_new / (1.0 - beta_one**STEP)
    scaled_second = second_new / (1.0 - beta_two**STEP)
    weight_new = weight - rate * (
        scaled_first / (jnp.sqrt(scaled_second) + epsilon) + decay * weight
    )
    return (weight_new, first_new, second_new)


def on_device(
    inputs,
    cotangent,
    qkv_weight,
    qkv_first,
    qkv_second,
    dense_weight,
    dense_first,
    dense_second,
    up_weight,
    up_first,
    up_second,
    down_weight,
    down_first,
    down_second,
    qkv_bias,
    qkv_bias_first,
    qkv_bias_second,
    up_bias,
    up_bias_first,
    up_bias_second,
    norm_vectors,
    norm_first,
    norm_second,
):
    rows = inputs.shape[0]
    group = rows * lax.axis_size("tensor")
    seq_count = group // LENGTH
    heads_local = qkv_weight.shape[2] // HEAD
    lowered = tuple(
        (
            member.astype(jnp.bfloat16)
            for member in (
                qkv_weight,
                dense_weight,
                up_weight,
                down_weight,
                qkv_bias,
                up_bias,
                norm_vectors,
            )
        )
    )
    qkv_full, dense_full, up_full, down_full, qkv_bias_full, up_bias_full, vectors_full = (
        lax.all_gather(lowered[0], "dp", axis=0, tiled=True),
        lax.all_gather(lowered[1], "dp", axis=0, tiled=True),
        lax.all_gather(lowered[2], "dp", axis=0, tiled=True),
        lax.all_gather(lowered[3], "dp", axis=0, tiled=True),
        lax.all_gather(lowered[4], "dp", axis=1, tiled=True),
        lax.all_gather(lowered[5], "dp", axis=0, tiled=True),
        lax.all_gather(lowered[6], "dp", axis=1, tiled=True),
    )
    vectors_wide = vectors_full.astype(jnp.float32)
    source = inputs.astype(jnp.float32)
    centered = source - jnp.mean(source, axis=1, keepdims=True)
    scale_inv = lax.rsqrt(jnp.mean(centered * centered, axis=1, keepdims=True) + norm_eps)
    unit = centered * scale_inv
    normed = (unit * vectors_wide[0] + vectors_wide[1]).astype(jnp.bfloat16)
    normed_all = lax.all_gather(normed, "tensor", axis=0, tiled=True)
    packed = jnp.einsum(
        "td,dcf->tcf", normed_all, qkv_full, preferred_element_type=jnp.float32
    ) + qkv_bias_full.astype(jnp.float32)
    positions = (jnp.arange(group, dtype=jnp.int32) % LENGTH).astype(jnp.float32)
    cosine, sine = angles(positions)
    query = rotate(packed[:, 0].reshape(group, heads_local, HEAD), cosine, sine).astype(
        jnp.bfloat16
    )
    keys = rotate(packed[:, 1].reshape(group, heads_local, HEAD), cosine, sine).astype(jnp.bfloat16)
    values = packed[:, 2].reshape(group, heads_local, HEAD).astype(jnp.bfloat16)
    seq_shape = (seq_count, LENGTH, heads_local, HEAD)
    query_seq = query.reshape(seq_shape)
    keys_seq = keys.reshape(seq_shape)
    values_seq = values.reshape(seq_shape)
    mixed, tops, totals = lax.map(attend_sequence, (query_seq, keys_seq, values_seq))
    attn_rows = mixed.reshape(group, heads_local * HEAD)
    hidden = jnp.dot(normed_all, up_full, preferred_element_type=jnp.float32) + up_bias_full.astype(
        jnp.float32
    )
    active = jax.nn.gelu(hidden, approximate=True).astype(jnp.bfloat16)
    partial_out = jnp.einsum("tf,of->to", attn_rows, dense_full, preferred_element_type=jnp.float32)
    partial_out = partial_out + jnp.einsum(
        "th,oh->to", active, down_full, preferred_element_type=jnp.float32
    )
    summed = lax.psum_scatter(partial_out, "tensor", scatter_dimension=0, tiled=True)
    output = (source + summed + vectors_wide[2] + vectors_wide[3]).astype(jnp.bfloat16)
    qkv_back, dense_back, up_back, down_back = (
        lax.all_gather(lowered[0], "dp", axis=0, tiled=True),
        lax.all_gather(lowered[1], "dp", axis=0, tiled=True),
        lax.all_gather(lowered[2], "dp", axis=0, tiled=True),
        lax.all_gather(lowered[3], "dp", axis=0, tiled=True),
    )
    grad_all = lax.all_gather(cotangent, "tensor", axis=0, tiled=True)
    dense_rows = jnp.einsum("to,tf->of", grad_all, attn_rows, preferred_element_type=jnp.float32)
    down_rows = jnp.einsum("to,th->oh", grad_all, active, preferred_element_type=jnp.float32)
    grad_active = jnp.dot(grad_all, down_back, preferred_element_type=jnp.float32)
    _, gelu_back = jax.vjp(partial(jax.nn.gelu, approximate=True), hidden)
    grad_hidden = gelu_back(grad_active)[0].astype(jnp.bfloat16)
    up_rows = jnp.einsum("td,th->dh", normed_all, grad_hidden, preferred_element_type=jnp.float32)
    up_bias_sum = jnp.sum(grad_hidden.astype(jnp.float32), axis=0)
    grad_mixed = jnp.dot(grad_all, dense_back, preferred_element_type=jnp.float32).astype(
        jnp.bfloat16
    )
    grad_query, grad_keys, grad_values = lax.map(
        attend_back, (query_seq, keys_seq, values_seq, grad_mixed.reshape(seq_shape), tops, totals)
    )
    flat_shape = (group, heads_local, HEAD)
    grad_query = rotate_back(grad_query.reshape(flat_shape), cosine, sine)
    grad_keys = rotate_back(grad_keys.reshape(flat_shape), cosine, sine)
    grad_values = grad_values.reshape(flat_shape)
    grad_packed = (
        jnp.stack([grad_query, grad_keys, grad_values], axis=1)
        .reshape(group, 3, heads_local * HEAD)
        .astype(jnp.bfloat16)
    )
    qkv_rows = jnp.einsum(
        "td,tcf->dcf", normed_all, grad_packed, preferred_element_type=jnp.float32
    )
    qkv_bias_sum = jnp.sum(grad_packed.astype(jnp.float32), axis=0)
    grad_normed = jnp.einsum(
        "tcf,dcf->td", grad_packed, qkv_back, preferred_element_type=jnp.float32
    )
    grad_normed = grad_normed + jnp.einsum(
        "th,dh->td", grad_hidden, up_back, preferred_element_type=jnp.float32
    )
    grad_normed_rows = lax.psum_scatter(
        grad_normed.astype(jnp.bfloat16), "tensor", scatter_dimension=0, tiled=True
    ).astype(jnp.float32)
    gain_sum = jnp.sum(grad_normed_rows * unit, axis=0)
    shift_sum = jnp.sum(grad_normed_rows, axis=0)
    grad_unit = grad_normed_rows * vectors_wide[0]
    grad_centered = scale_inv * (
        grad_unit
        - jnp.mean(grad_unit, axis=1, keepdims=True)
        - unit * jnp.mean(grad_unit * unit, axis=1, keepdims=True)
    )
    grad_out = cotangent.astype(jnp.float32)
    input_grad = grad_out + grad_centered
    bias_sum = jnp.sum(grad_out, axis=0)
    vector_rows = jnp.stack([gain_sum, shift_sum, bias_sum, bias_sum])
    (
        qkv_summed,
        dense_summed,
        up_summed,
        down_summed,
        qkv_bias_summed,
        up_bias_summed,
        vector_part,
    ) = (
        lax.psum_scatter(qkv_rows, "dp", scatter_dimension=0, tiled=True),
        lax.psum_scatter(dense_rows, "dp", scatter_dimension=0, tiled=True),
        lax.psum_scatter(up_rows, "dp", scatter_dimension=0, tiled=True),
        lax.psum_scatter(down_rows, "dp", scatter_dimension=0, tiled=True),
        lax.psum_scatter(qkv_bias_sum, "dp", scatter_dimension=1, tiled=True),
        lax.psum_scatter(up_bias_sum, "dp", scatter_dimension=0, tiled=True),
        lax.psum_scatter(vector_rows, "dp", scatter_dimension=1, tiled=True),
    )
    vector_summed = lax.psum(vector_part, "tensor")
    grads = (
        qkv_summed,
        dense_summed,
        up_summed,
        down_summed,
        qkv_bias_summed,
        up_bias_summed,
        vector_summed,
    )
    weights = (qkv_weight, dense_weight, up_weight, down_weight, qkv_bias, up_bias, norm_vectors)
    firsts = (
        qkv_first,
        dense_first,
        up_first,
        down_first,
        qkv_bias_first,
        up_bias_first,
        norm_first,
    )
    seconds = (
        qkv_second,
        dense_second,
        up_second,
        down_second,
        qkv_bias_second,
        up_bias_second,
        norm_second,
    )
    rates = (0.02, 0.02, 0.02, 0.02, 0.2, 0.2, 0.2)
    decays = (0.1, 0.1, 0.1, 0.1, 0.0, 0.0, 0.0)
    results = [output, input_grad]
    for index in range(7):
        weight_new, first_new, second_new = adam(
            weights[index], grads[index], firsts[index], seconds[index], rates[index], decays[index]
        )
        results += [grads[index], weight_new, first_new, second_new]
    return tuple(results)


def solution(mesh):
    in_specs = (
        P(("dp", "tensor"), None),
        P(("dp", "tensor"), None),
        P("dp", None, "tensor"),
        P("dp", None, "tensor"),
        P("dp", None, "tensor"),
        P("dp", "tensor"),
        P("dp", "tensor"),
        P("dp", "tensor"),
        P("dp", "tensor"),
        P("dp", "tensor"),
        P("dp", "tensor"),
        P("dp", "tensor"),
        P("dp", "tensor"),
        P("dp", "tensor"),
        P(None, ("tensor", "dp")),
        P(None, ("tensor", "dp")),
        P(None, ("tensor", "dp")),
        P(("tensor", "dp")),
        P(("tensor", "dp")),
        P(("tensor", "dp")),
        P(None, "dp"),
        P(None, "dp"),
        P(None, "dp"),
    )
    out_specs = (
        P(("dp", "tensor"), None),
        P(("dp", "tensor"), None),
        P("dp", None, "tensor"),
        P("dp", None, "tensor"),
        P("dp", None, "tensor"),
        P("dp", None, "tensor"),
        P("dp", "tensor"),
        P("dp", "tensor"),
        P("dp", "tensor"),
        P("dp", "tensor"),
        P("dp", "tensor"),
        P("dp", "tensor"),
        P("dp", "tensor"),
        P("dp", "tensor"),
        P("dp", "tensor"),
        P("dp", "tensor"),
        P("dp", "tensor"),
        P("dp", "tensor"),
        P(None, ("tensor", "dp")),
        P(None, ("tensor", "dp")),
        P(None, ("tensor", "dp")),
        P(None, ("tensor", "dp")),
        P(("tensor", "dp")),
        P(("tensor", "dp")),
        P(("tensor", "dp")),
        P(("tensor", "dp")),
        P(None, "dp"),
        P(None, "dp"),
        P(None, "dp"),
        P(None, "dp"),
    )
    return jax.shard_map(
        on_device, mesh=mesh, in_specs=in_specs, out_specs=out_specs, check_vma=False
    )
```

profile of v0, /device:TPU:0, one launch (start us, length us, event | category | flops | bytes accessed | tf_op | source)
XLA Modules:
  0.0 1746.4 jit_solution(17164074992637337780)
XLA Ops:
  11.2 27.8 %all_gather.31 = bf16[4,2048]{1,0:T(4,128)(2,1)S(1)} all-gather(bf16[4,256]{1,0:T(4,128)(2,1)S(1)} %convert_element_type.123), channel_id=1, replica_groups=mesh['dp'=8,'tensor'=4] {'dp'}, dimensions={1}, use_global_device_ids=true | all-gather | bytes 18432 | tf_op jit(solution)/shard_map/all_gather | solution.py:190
  47.0 19.0 %all-gather.1 = bf16[8,1,256]{2,1,0:T(2,128)(2,1)S(1)} all-gather(bf16[1,1,256]{2,1,0:T(2,128)(2,1)S(1)} %reshape.245), channel_id=1, replica_groups=mesh['dp'=8,'tensor'=4] {'dp'}, dimensions={0}, use_global_device_ids=true | all-gather | bytes 4608 | tf_op jit(solution)/shard_map/all_gather | solution.py:189
  66.0 11.0 all-gather.9.cloned.1.call-done
  77.0 127.7 %all-gather.15.cloned.1.call-done = bf16[2048,2048]{1,0:T(8,128)(2,1)} async-done(((bf16[256,2048]{1,0:T(8,128)(2,1)}), bf16[2048,2048]{1,0:T(8,128)(2,1)}) %all-gather.15.cloned.1.call-update) | async-done | bytes 8388624 | tf_op jit(solution)/shard_map/all_gather | solution.py:186
  204.6 14.6 fusion.78
  219.2 19.7 %all-gather.19.cloned.1.call-done = bf16[1024,2048]{1,0:T(8,128)(2,1)} async-done(((bf16[256,2048]{1,0:T(8,128)(2,1)}), bf16[1024,2048]{1,0:T(8,128)(2,1)}) %all-gather.19.cloned.1.call-update) | async-done | bytes 4194320 | tf_op jit(solution)/shard_map/all_gather | solution.py:231
  238.9 16.9 convolution_bitcast_fusion
  256.5 32.0 %all-gather = bf16[8,64,3]{1,2,0:T(4,128)(2,1)S(1)} all-gather(bf16[1,64,3]{1,2,0:T(4,128)(2,1)S(1)} %convert_bitcast_fusion), channel_id=1, replica_groups=mesh['dp'=8,'tensor'=4] {'dp'}, dimensions={0}, use_global_device_ids=true | all-gather | bytes 3456 | tf_op jit(solution)/shard_map/all_gather | solution.py:188
  290.9 6.2 convolution_convert_fusion
  297.1 94.7 %all-gather.11.cloned.1.call-done = bf16[2048,3,512]{0,2,1:T(8,128)(2,1)} async-done(((bf16[256,3,512]{0,2,1:T(8,128)(2,1)}), bf16[2048,3,512]{0,2,1:T(8,128)(2,1)}) %all-gather.11.cloned.1.call-update) | async-done | bytes 6291472 | tf_op jit(solution)/shard_map/all_gather | solution.py:184
  391.9 10.1 broadcast_add_fusion
  405.3 38.3 %while.51 = (s32[]{:T(128)}, bf16[2,512,8,64]{1,3,2,0:T(8,128)(2,1)}, f32[2,8,512,1]{2,1,3,0:T(8,128)S(1)}, f32[2,8,512,1]{2,1,3,0:T(8,128)S(1)}, s32[2]{0:T(128...) while((s32[]{:T(128)}, ...), condition=%wide.region_5.6_spmd, body=%wide.region_2.5_spmd.sunk | while | flops 1124852224 | bytes 55726256 | solution.py:85
  408.9 4.7 fusion.124
  417.9 6.6 fusion.126
  428.0 4.7 fusion.124
  436.9 6.7 fusion.126
  443.6 233.0 %reduce-scatter.23.cloned.1.call-done = f32[256,2048]{1,0:T(8,128)} async-done(((f32[2048,2048]{1,0:T(8,128)}), f32[256,2048]{1,0:T(8,128)}) %reduce-scatter.23.cloned.1.call-update) | async-done | bytes 2097168 | tf_op jit(solution)/shard_map/reduce_scatter | solution.py:291
  676.7 8.6 multiply_subtract_fusion
  685.3 150.3 %while.52 = (s32[]{:T(128)}, f32[1024,8,64]{0,2,1:T(8,128)S(1)}, f32[1024,8,64]{0,2,1:T(8,128)}, f32[2,512,8,64]{1,0,3,2:T(2,128)}, s32[2]{0:T(128)S(1)}, /*inde...) while((s32[]{:T(128)}, f32[1024,8,64]{0,2,1:T(8,128)S(1)}, ...), condition=%wide.region_9.10_spmd.clone, body=%wide.region_7.9_spmd.clone.sunk | while | flops 2729701888 | bytes 150081792 | solution.py:125
  689.3 9.8 fusion.136
  699.1 13.6 multiply_reduce_fusion.2
  712.7 11.5 multiply_convert_fusion.5
  724.3 8.7 bitcast_add_fusion.6
  740.9 19.7 %dynamic_update_slice.39 = f32[2,512,8,64]{1,0,3,2:T(2,128)} dynamic-update-slice(f32[2,512,8,64]{1,0,3,2:T(2,128)} %get-tuple-element.628, f32[1,512,8,64]{1,0,3,2:T(1,128)} %copy.144, s32[]{:T(128)S(6)} %copy.165, s32[]{:T(128)} %constant.78.clone.1..sunk.1, s32[]{:T(128)} %constant.78.clone.1..sunk.1, s32[]{:T(128)} %constant.78.clone.1..sunk.1) | dynamic-update-slice | bytes 2097156 | tf_op jit(solution)/shard_map/while/body/eval_jaxpr/while/body/jit(dynamic_update_index_in_dim)/dynamic_update_slice | solution.py:125
  764.1 9.6 fusion.136
  773.8 13.6 multiply_reduce_fusion.2
  787.4 11.4 multiply_convert_fusion.5
  798.8 9.3 bitcast_add_fusion.6
  815.8 19.6 %dynamic_update_slice.39 = f32[2,512,8,64]{1,0,3,2:T(2,128)} dynamic-update-slice(f32[2,512,8,64]{1,0,3,2:T(2,128)} %get-tuple-element.628, f32[1,512,8,64]{1,0,3,2:T(1,128)} %copy.144, s32[]{:T(128)S(6)} %copy.165, s32[]{:T(128)} %constant.78.clone.1..sunk.1, s32[]{:T(128)} %constant.78.clone.1..sunk.1, s32[]{:T(128)} %constant.78.clone.1..sunk.1) | dynamic-update-slice | bytes 2097156 | tf_op jit(solution)/shard_map/while/body/eval_jaxpr/while/body/jit(dynamic_update_index_in_dim)/dynamic_update_slice | solution.py:125
  850.1 18.8 %convert_reduce_fusion = (f32[2048]{0:T(1024)S(1)}, bf16[1024,2048]{1,0:T(8,128)(2,1)S(1)}) fusion(f32[1024,2048]{1,0:T(8,128)} %fusion.78, f32[2048]{0:T(1024)S(1)} %bitcast.154, bf16[1024,2048]{1,0:T(8,128)(2,1)} %all-gather.19.cloned.1.call-done, bf16[2048,2048]{1,0:T(8,128)(2,1)} %all-gather.17.cloned.1.call-done), kind=kOutput, calls=%fused_computation.52 | convolution fusion | flops 8638167040 | bytes 25182208 | tf_op jit(solution)/shard_map/dot_general | solution.py:234
  868.9 12.8 fusion.79
  881.8 11.0 fusion.32
  895.4 17.8 %fusion.67 = f32[1024,2048]{1,0:T(8,128)S(1)} fusion(bf16[2048,2048]{1,0:T(8,128)(2,1)} %all-gather.17.cloned.1.call-done, f32[1024,2048]{1,0:T(8,128)} %fusion.78, f32[2048]{0:T(1024)S(1)} %bitcast.155), kind=kOutput, calls=%fused_computation.151 | convolution fusion | flops 8610906112 | bytes 25174016 | tf_op jit(solution)/shard_map/th,oh->to/dot_general | solution.py:220
  913.3 5.7 convolution_add_fusion
  921.7 6.6 convolution_bitcast_fusion.1
  929.5 11.7 fusion.33
  944.7 66.5 %reduce-scatter.13.cloned.1.call-done = f32[256,2048]{1,0:T(8,128)} async-done(((f32[1024,2048]{1,0:T(8,128)}), f32[256,2048]{1,0:T(8,128)}) %reduce-scatter.13.cloned.1.call-update) | async-done | bytes 2097168 | tf_op jit(solution)/shard_map/reduce_scatter | solution.py:223
  1011.3 5.1 convert_reduce_fusion.4
  1017.8 15.3 fusion.80
  1036.1 40.6 %reduce-scatter.25.cloned.1.call-done = f32[64,3]{1,0:T(8,128)} async-done(((f32[512,3]{1,0:T(8,128)}), f32[64,3]{1,0:T(8,128)}) %reduce-scatter.25.cloned.1.call-update) | async-done | bytes 784
  1078.1 89.9 %reduce-scatter.19.cloned.1.call-done = f32[256,512]{0,1:T(8,128)} async-done(((f32[2048,512]{0,1:T(8,128)}), f32[256,512]{0,1:T(8,128)}) %reduce-scatter.19.cloned.1.call-update) | async-done | bytes 524304 | tf_op jit(solution)/shard_map/reduce_scatter | solution.py:289
  1175.4 204.2 %reduce-scatter.17.cloned.1.call-done = f32[256,3,512]{2,0,1:T(8,128)} async-done(((f32[2048,3,512]{2,0,1:T(8,128)}), f32[256,3,512]{2,0,1:T(8,128)}) %reduce-scatter.17.cloned.1.call-update) | async-done | bytes 1572880 | tf_op jit(solution)/shard_map/reduce_scatter | solution.py:288
  1379.6 5.9 multiply_subtract_fusion.2
  1385.5 20.1 %all-reduce = f32[2048]{0:T(1024)S(1)} all-reduce(f32[2048]{0:T(1024)S(1)} %get-tuple-element.395), channel_id=9, replica_groups=mesh['dp'=8,'tensor'=4] {'dp'}, use_global_device_ids=true, to_apply=%region_20.21.clone | all-reduce | flops 2048 | bytes 16384
  1406.3 40.4 %reduce-scatter.27.cloned.1.call-done = f32[256,4]{1,0:T(8,128)} async-done(((f32[2048,4]{1,0:T(8,128)}), f32[256,4]{1,0:T(8,128)}) %reduce-scatter.27.cloned.1.call-update) | async-done | bytes 4112
  1447.7 5.6 psum.7
  1454.0 278.8 %reduce-scatter.21.cloned.1.call-done = f32[256,2048]{1,0:T(8,128)} async-done(((f32[2048,2048]{1,0:T(8,128)}), f32[256,2048]{1,0:T(8,128)}) %reduce-scatter.21.cloned.1.call-update) | async-done | bytes 2097168 | tf_op jit(solution)/shard_map/reduce_scatter | solution.py:290
  1732.8 6.9 multiply_subtract_fusion.1
  (214 shorter events, 87.8 us)
Async XLA Ops:
  7.2 35.8 %copy-start.3 = (f32[256,2048]{1,0:T(8,128)S(1)}, f32[256,2048]{1,0:T(8,128)}, u32[]{:S(2)}) copy-start(f32[256,2048]{1,0:T(8,128)} %param.35) | copy-start | bytes 6291460
  7.2 69.8 %all-gather.9.cloned.1.call-start = ((), (), s32[]{:S(2)}) async-start(), calls=%async_computation.8 | async-start | bytes 5242880 | tf_op jit(solution)/shard_map/all_gather | solution.py:198
  8.9 30.8 %copy-start.25 = (f32[256]{0:T(256)}, f32[256]{0:T(256)S(1)}, u32[]{:S(2)}) copy-start(f32[256]{0:T(256)S(1)} %broadcast_multiply_fusion.2) | copy-start | bytes 3076
  10.5 29.1 %copy-start.29 = (f32[256]{0:T(256)}, f32[256]{0:T(256)S(1)}, u32[]{:S(2)}) copy-start(f32[256]{0:T(256)S(1)} %add_rsqrt_fusion) | copy-start | bytes 3076
  42.9 2.0 copy-start.11
  42.9 161.7 %all-gather.15.cloned.1.call-start = ((), (), s32[]{:S(2)}) async-start(), calls=%async_computation.11 | async-start | bytes 9437184 | tf_op jit(solution)/shard_map/all_gather | solution.py:186
  44.1 2.9 copy-start.40
  44.1 194.8 %all-gather.19.cloned.1.call-start = ((), (), s32[]{:S(2)}) async-start(), calls=%async_computation.14 | async-start | bytes 5242880 | tf_op jit(solution)/shard_map/all_gather | solution.py:231
  44.8 246.1 %all-gather.13.cloned.1.call-start = ((), (), s32[]{:S(2)}) async-start(), calls=%async_computation.10 | async-start | bytes 2359296 | tf_op jit(solution)/shard_map/all_gather | solution.py:185
  45.7 346.2 %all-gather.11.cloned.1.call-start = ((), (), s32[]{:S(2)}) async-start(), calls=%async_computation.9 | async-start | bytes 7077888 | tf_op jit(solution)/shard_map/all_gather | solution.py:184
  46.9 629.8 %reduce-scatter.23.cloned.1.call-start = ((), (), s32[]{:S(2)}) async-start(), calls=%async_computation.19 | async-start | bytes 18874368 | tf_op jit(solution)/shard_map/reduce_scatter | solution.py:291
  66.0 172.9 %copy-start.34 = (f32[8,1,256]{2,1,0:T(1,128)}, f32[8,1,256]{2,1,0:T(1,128)S(1)}, u32[]{:S(2)}) copy-start(f32[8,1,256]{2,1,0:T(1,128)S(1)} %convert_element_type.146) | copy-start | bytes 24580
  255.8 594.3 %all-gather.17.cloned.1.call-start = ((), (), s32[]{:S(2)}) async-start(), calls=%async_computation.12 | async-start | bytes 9437184 | tf_op jit(solution)/shard_map/all_gather | solution.py:187
  288.9 114.9 %copy-start.15 = (f32[1024,16]{0,1:T(8,128)}, f32[1024,16]{0,1:T(8,128)S(1)}, u32[]{:S(2)}) copy-start(f32[1024,16]{0,1:T(8,128)S(1)} %get-tuple-element.442) | copy-start | bytes 196612
  288.9 114.9 %copy-start.17 = (f32[1024,16]{0,1:T(8,128)}, f32[1024,16]{0,1:T(8,128)S(1)}, u32[]{:S(2)}) copy-start(f32[1024,16]{0,1:T(8,128)S(1)} %get-tuple-element.443) | copy-start | bytes 196612
  443.6 241.7 %copy-start = (f32[1024,8,64]{0,2,1:T(8,128)S(1)}, f32[1024,8,64]{0,2,1:T(8,128)}, u32[]{:S(2)}) copy-start(f32[1024,8,64]{0,2,1:T(8,128)} %custom-call) | copy-start | bytes 6291460
  685.2 256.3 %reduce-scatter.15.cloned.1.call-start = ((), (), s32[]{:S(2)}) async-start(), calls=%async_computation.15 | async-start | bytes 5242880 | tf_op jit(solution)/shard_map/reduce_scatter | solution.py:264
  712.7 11.6 copy-start.1
  787.4 11.4 copy-start.1
  835.6 6.2 copy-start.16
  835.7 6.2 copy-start.18
  845.8 4.3 copy-start.35
  850.1 31.7 %copy-start.6 = (bf16[1024,1,512]{2,0,1:T(8,128)(2,1)}, bf16[1024,1,512]{2,0,1:T(8,128)(2,1)S(1)}, u32[]{:S(2)}) copy-start(bf16[1024,1,512]{2,0,1:T(8,128)(2,1)S(1)} %copy.110) | copy-start | bytes 3145732
  868.9 12.8 copy-start.45
  892.8 118.5 %reduce-scatter.13.cloned.1.call-start = ((), (), s32[]{:S(2)}) async-start(), calls=%async_computation.13 | async-start | bytes 10485760 | tf_op jit(solution)/shard_map/reduce_scatter | solution.py:223
  895.4 17.8 %copy-start.9 = (bf16[2048,512]{1,0:T(8,128)(2,1)S(1)}, bf16[2048,512]{1,0:T(8,128)(2,1)}, u32[]{:S(2)}) copy-start(bf16[2048,512]{1,0:T(8,128)(2,1)} %all-gather.13.cloned.1.call-done) | copy-start | bytes 6291460
  919.0 157.7 %reduce-scatter.25.cloned.1.call-start = ((), (), s32[]{:S(2)}) async-start(), calls=%async_computation.20 | async-start | bytes 294912
  921.6 246.4 %reduce-scatter.19.cloned.1.call-start = ((), (), s32[]{:S(2)}) async-start(), calls=%async_computation.17 | async-start | bytes 4718592 | tf_op jit(solution)/shard_map/reduce_scatter | solution.py:289
  928.3 451.4 %reduce-scatter.17.cloned.1.call-start = ((), (), s32[]{:S(2)}) async-start(), calls=%async_computation.16 | async-start | bytes 14155776 | tf_op jit(solution)/shard_map/reduce_scatter | solution.py:288
  941.2 70.1 %copy-start.8 = (bf16[256,2048]{1,0:T(8,128)(2,1)S(1)}, bf16[256,2048]{1,0:T(8,128)(2,1)}, u32[]{:S(2)}) copy-start(bf16[256,2048]{1,0:T(8,128)(2,1)} %param.28) | copy-start | bytes 3145732
  941.2 70.0 %copy-start.23 = (f32[1,2048]{1,0:T(1,128)S(1)}, f32[1,2048]{1,0:T(1,128)}, u32[]{:S(2)}) copy-start(f32[1,2048]{1,0:T(1,128)} %get-tuple-element.438) | copy-start | bytes 24580
  941.2 70.0 %copy-start.24 = (f32[1,2048]{1,0:T(1,128)S(1)}, f32[1,2048]{1,0:T(1,128)}, u32[]{:S(2)}) copy-start(f32[1,2048]{1,0:T(1,128)} %get-tuple-element.439) | copy-start | bytes 24580
  941.3 505.4 %reduce-scatter.27.cloned.1.call-start = ((), (), s32[]{:S(2)}) async-start(), calls=%async_computation.21 | async-start | bytes 1179648
  1017.7 715.0 %reduce-scatter.21.cloned.1.call-start = ((), (), s32[]{:S(2)}) async-start(), calls=%async_computation.18 | async-start | bytes 18874368 | tf_op jit(solution)/shard_map/reduce_scatter | solution.py:290
  1033.2 1.7 copy-start.44
  1033.2 44.3 %copy-start.33 = (f32[3,64]{1,0:T(4,128)S(1)}, f32[3,64]{1,0:T(4,128)}, u32[]{:S(2)}) copy-start(f32[3,64]{1,0:T(4,128)} %param.41) | copy-start | bytes 2308
  1033.2 44.3 %copy-start.38 = (f32[3,64]{1,0:T(4,128)S(1)}, f32[3,64]{1,0:T(4,128)}, u32[]{:S(2)}) copy-start(f32[3,64]{1,0:T(4,128)} %param.42) | copy-start | bytes 2308
  1033.2 44.3 %copy-start.39 = (f32[3,64]{1,0:T(4,128)S(1)}, f32[3,64]{1,0:T(4,128)}, u32[]{:S(2)}) copy-start(f32[3,64]{1,0:T(4,128)} %param.43) | copy-start | bytes 2308
  1077.5 96.9 %copy-start.31 = (f32[3,64]{1,0:T(4,128)}, f32[3,64]{1,0:T(4,128)S(1)}, u32[]{:S(2)}) copy-start(f32[3,64]{1,0:T(4,128)S(1)} %copy.127) | copy-start | bytes 2308
  1168.1 6.3 copy-start.10
  1175.4 230.2 %copy-start.41 = (f32[256]{0:T(256)S(1)}, f32[256]{0:T(256)}, u32[]{:S(2)}) copy-start(f32[256]{0:T(256)} %param.44) | copy-start | bytes 3076
  1175.4 230.2 %copy-start.42 = (f32[256]{0:T(256)S(1)}, f32[256]{0:T(256)}, u32[]{:S(2)}) copy-start(f32[256]{0:T(256)} %param.45) | copy-start | bytes 3076
  1175.4 230.3 %copy-start.43 = (f32[256]{0:T(256)S(1)}, f32[256]{0:T(256)}, u32[]{:S(2)}) copy-start(f32[256]{0:T(256)} %param.46) | copy-start | bytes 3076
  1175.4 277.9 %copy-start.27 = (f32[4,256]{1,0:T(4,128)S(1)}, f32[4,256]{1,0:T(4,128)}, u32[]{:S(2)}) copy-start(f32[4,256]{1,0:T(4,128)} %param.47) | copy-start | bytes 12292
  1175.4 277.9 %copy-start.36 = (f32[4,256]{1,0:T(4,128)S(1)}, f32[4,256]{1,0:T(4,128)}, u32[]{:S(2)}) copy-start(f32[4,256]{1,0:T(4,128)} %param.48) | copy-start | bytes 12292
  1175.4 277.9 %copy-start.37 = (f32[4,256]{1,0:T(4,128)S(1)}, f32[4,256]{1,0:T(4,128)}, u32[]{:S(2)}) copy-start(f32[4,256]{1,0:T(4,128)} %param.49) | copy-start | bytes 12292
  1175.4 557.3 %copy-start.4 = (f32[256,2048]{1,0:T(8,128)S(1)}, f32[256,2048]{1,0:T(8,128)}, u32[]{:S(2)}) copy-start(f32[256,2048]{1,0:T(8,128)} %param.35) | copy-start | bytes 6291460
  1453.4 286.3 %copy-start.28 = (f32[4,256]{1,0:T(4,128)}, f32[4,256]{1,0:T(4,128)S(1)}, u32[]{:S(2)}) copy-start(f32[4,256]{1,0:T(4,128)S(1)} %psum.7) | copy-start | bytes 12292
  (13 other events, 14.9 us)
Sparse Core Ops, SparseCore 0:
  43.0 33.9 all-gather.8
  79.7 124.9 all-gather.14
  206.2 32.6 all-gather.18
  241.5 49.4 all-gather.12
  293.4 98.4 all-gather.10
  396.1 280.5 reduce-scatter.22
  685.4 123.9 all-gather.16
  892.9 43.9 reduce-scatter.14
  939.5 71.7 reduce-scatter.12
  1015.4 61.2 reduce-scatter.24
  1080.7 87.2 reduce-scatter.18
  1172.1 207.4 reduce-scatter.16
  1383.6 63.0 reduce-scatter.26
  1451.4 281.3 reduce-scatter.20
where the time goes:
time: 1760 us; the launch traced here: 1750 us
  waiting for transfers between devices  1210 us (69%)
  matrix products  246 us (14%)
  blocking collectives  104 us (6%)
  other arithmetic  85.5 us (5%)
  local copies, waits for them, and re-layouts  75.8 us (4%)
    reduce_scatter x1, waiting for transfers between devices, on_device(): lax.psum_scatter(up_rows, 'dp', scatter_dimension=0, tiled=True)  279 us
    reduce_scatter x1, waiting for transfers between devices, on_device(): lax.psum_scatter(down_rows, 'dp', scatter_dimension=0, tiled=True)  233 us
    reduce_scatter x1, waiting for transfers between devices, on_device(): lax.psum_scatter(qkv_rows, 'dp', scatter_dimension=0, tiled=True)  204 us
    all_gather x1, waiting for transfers between devices, on_device(): lax.all_gather(lowered[2], 'dp', axis=0, tiled=True)  128 us
    all_gather x1, waiting for transfers between devices, on_device(): lax.all_gather(lowered[0], 'dp', axis=0, tiled=True)  94.7 us
    reduce_scatter x1, waiting for transfers between devices, on_device(): lax.psum_scatter(dense_rows, 'dp', scatter_dimension=0, tiled=True)  89.9 us
    unnamed x16, waiting for transfers between devices  81.9 us
    reduce_scatter x1, waiting for transfers between devices, on_device(): lax.psum_scatter(partial_out, 'tensor', scatter_dimension=0, tiled=True)  66.5 us
  transfers between devices with their start and end apart: 14, of which 12 were waited for; matrix products, arithmetic and copies ran while one was open for 19% of the time, Pallas kernels for 0%

commit v1 on v0

v1 whole, which is shorter than its diff:
```python
from functools import partial

import jax
import jax.numpy as jnp
import numpy as np
from jax import lax
from jax.experimental import pallas as pl
from jax.experimental.pallas import tpu as pltpu
from jax.sharding import Mesh
from jax.sharding import PartitionSpec as P

HEAD = 64
ROT = 32
LENGTH = 1024
STEP = 10
BLOCK = 256

norm_eps = 1e-05
beta_one = 0.9
beta_two = 0.999
epsilon = 1e-08
masked = -1e30
f32 = jnp.float32
bf16 = jnp.bfloat16


def ordered(index, own, other, axis):
    first = jnp.where(index == 0, own, other)
    second = jnp.where(index == 0, other, own)
    return jnp.concatenate([first, second], axis=axis)


def pick(value, index, axis):
    return lax.dynamic_index_in_dim(value, index, axis, keepdims=False)


MESH = pl.DeviceIdType.MESH


def here():
    return tuple(lax.axis_index(name) for name in ("z", "x", "y", "c"))


def remote(source, target, send, recv, device):
    return pltpu.make_async_remote_copy(
        src_ref=source,
        dst_ref=target,
        send_sem=send,
        recv_sem=recv,
        device_id=device,
        device_id_type=MESH,
    )


def span(start, size):
    return pl.ds(pl.multiple_of(start, 16), size)


class Tokens:
    def __init__(self, own, full, send, recv, local):
        self.own, self.full, self.send, self.recv, self.local = own, full, send, recv, local
        self.rows = own.shape[0]

    def at(self, x, y, c, part=None):
        start = ((x * 2 + y) * 2 + c) * self.rows
        cut = self.rows * 5 // 8
        if part is None:
            return self.full.at[span(start, self.rows)]
        return self.full.at[span(start + part * cut, self.rows - cut if part else cut)]

    def copy(self, index, arrives=False):
        _, x, y, c = here()
        to_x, to_y, to_c = {"x": 1 - x}, {"y": 1 - y}, {"c": 1 - c}
        owner, part, device, other = (
            ((x, y, c), None, to_x, (1 - x, y, c)),
            ((x, y, c), None, to_y, (x, 1 - y, c)),
            ((x, y, c), None, to_c, (x, y, 1 - c)),
            ((1 - x, y, c), 0, to_y, (1 - x, 1 - y, c)),
            ((1 - x, y, c), None, to_c, (1 - x, y, 1 - c)),
            ((x, 1 - y, c), 1, to_x, (1 - x, 1 - y, c)),
            ((x, 1 - y, c), None, to_c, (x, 1 - y, 1 - c)),
            ((1 - x, 1 - y, c), 0, to_c, (1 - x, 1 - y, 1 - c)),
            ((1 - x, 1 - y, c), 1, to_c, (1 - x, 1 - y, 1 - c)),
        )[index]
        target = self.at(*(other if arrives else owner), part)
        source = self.own if index < 3 else target
        return remote(source, target, self.send.at[index], self.recv.at[index], device)

    def own_copy(self):
        _, x, y, c = here()
        return pltpu.make_async_copy(self.own, self.at(x, y, c), self.local)

    def begin(self):
        self.own_copy().start()
        for index in range(3):
            self.copy(index).start()

    def middle(self):
        for first, index in ((0, 3), (1, 5)):
            self.copy(first, arrives=True).wait_recv()
            self.copy(index).start()
            self.copy(index + 1).start()

    def late(self):
        for first, index in ((3, 7), (5, 8)):
            self.copy(first, arrives=True).wait_recv()
            self.copy(index).start()

    def end(self):
        for index in (2, 4, 6, 7, 8):
            self.copy(index, arrives=True).wait_recv()
        for index in range(9):
            self.copy(index).wait_send()
        self.own_copy().wait()


class Line:
    def __init__(self, steps, halves, full, swap_sem, send, recv, local):
        self.steps, self.halves, self.full = steps, halves, full
        self.swap_sem, self.send, self.recv, self.local = swap_sem, send, recv, local
        self.rows = halves.shape[1]

    def at(self, z, x):
        return self.full.at[span((z * 2 + x) * self.rows, self.rows)]

    def own_copy(self):
        z, x, _, _ = here()
        return pltpu.make_async_copy(self.halves.at[x], self.at(z, x), self.local)

    def swap(self, arrives=False):
        z, x, _, _ = here()
        target = self.at(z, 1 - x if arrives else x)
        return remote(
            self.halves.at[1 - x], target, self.swap_sem.at[0], self.swap_sem.at[1], {"x": 1 - x}
        )

    def hop(self, step, which, way, arrives=False):
        z, x, _, _ = here()
        owner = z - step if way == 0 else z + step
        side = x if which == 0 else 1 - x
        device = {"z": jnp.clip(z + 1 if way == 0 else z - 1, 0, self.steps - 1)}
        owner = jnp.clip(owner, 0, self.steps - 1)
        target = self.at(owner, side)
        source = self.halves.at[x] if step == 0 and which == 0 else target
        index = (step - 1 if arrives else step) * 4 + which * 2 + way
        return remote(source, target, self.send.at[index], self.recv.at[index], device)

    def has(self, step, way):
        z = here()[0]
        return z >= step if way == 0 else z + step < self.steps

    def sends(self, step, way):
        z = here()[0]
        last = z < self.steps - 1 if way == 0 else z > 0
        return jnp.logical_and(self.has(step, way), last)

    def begin(self):
        self.own_copy().start()
        self.swap().start()
        self.push(0, 0)

    def push(self, step, which):
        if step < self.steps - 1:
            for way in (0, 1):

                @pl.when(self.sends(step, way))
                def _():
                    self.hop(step, which, way).start()

    def swapped(self):
        self.swap(arrives=True).wait_recv()
        self.push(0, 1)

    def turn(self, step, which):
        for way in (0, 1):

            @pl.when(self.has(step, way))
            def _():
                self.hop(step, which, way, arrives=True).wait_recv()

            if step < self.steps - 1:

                @pl.when(self.sends(step, way))
                def _():
                    self.hop(step, which, way).start()

    def end(self):
        self.own_copy().wait()
        self.swap().wait_send()
        for step in range(self.steps - 1):
            for which in (0, 1):
                for way in (0, 1):

                    @pl.when(self.sends(step, way))
                    def _():
                        self.hop(step, which, way).wait_send()


class SmallSum:
    def __init__(self, steps, mine, out, got, near_got, send, recv):
        self.steps, self.mine, self.out, self.got = steps, mine, out, got
        self.near_got, self.send, self.recv = near_got, send, recv

    def copy(self, k, arrives=False):
        z, x, _, _ = here()
        shards = self.steps * 2
        me = z * 2 + x
        other = lax.rem(me + k, shards)
        device = {"z": other // 2, "x": lax.rem(other, 2)}
        slot = other if arrives else me
        return remote(
            self.mine.at[other], self.got.at[slot], self.send.at[k], self.recv.at[slot], device
        )

    def each(self, act):
        def body(k, carry):
            act(k)
            return carry

        lax.fori_loop(1, self.steps * 2, body, 0)

    def begin(self):
        z, x, _, _ = here()
        self.each(lambda k: self.copy(k).start())
        self.got[z * 2 + x] = self.mine[z * 2 + x]

    def finish(self):
        _, _, y, c = here()
        shards = self.steps * 2
        self.each(lambda k: self.copy(k, arrives=True).wait_recv())
        total = self.got[0]
        for shard in range(1, shards):
            total = total + self.got[shard]
        self.out[...] = total
        half = total.shape[0] // 2
        at = y * 2 + c
        self.near_got[at] = total[:half]
        copies = []
        for index, (other_y, other_c) in enumerate(((y, 1 - c), (1 - y, c), (1 - y, 1 - c))):
            there = other_y * 2 + other_c
            sems = (self.send.at[shards + index], self.recv.at[shards + index])
            device = {"y": other_y, "c": other_c}
            leave = remote(self.near_got.at[at], self.near_got.at[at], *sems, device)
            leave.start()
            arrive = remote(self.near_got.at[there], self.near_got.at[there], *sems, device)
            copies.append((leave, arrive))
        for _, arrive in copies:
            arrive.wait_recv()
        near = self.near_got
        self.out[:half] = (near[0] + near[1]) + (near[2] + near[3])
        for leave, _ in copies:
            leave.wait_send()
        self.each(lambda k: self.copy(k).wait_send())


class SmallSizes:
    def __init__(self, norm, bias, up):
        self.norm, self.bias, self.up = norm, bias, up
        self.across = min(128, norm)
        self.norm_lines = norm // self.across


def put_lines(target, shard, row, line, start, size):
    wide = min(128, size)
    for index in range(size // wide):
        at = start + index * wide
        target[shard, row + index : row + index + 1, :wide] = line[:, at : at + wide]


def greet_wide(steps):
    z, x, y, c = here()
    shards = steps * 2
    barrier = pltpu.get_barrier_semaphore()

    def greet(k, carry):
        other = lax.rem(z * 2 + x + k, shards)
        device = {"z": other // 2, "x": lax.rem(other, 2)}
        pl.semaphore_signal(barrier, inc=1, device_id=device, device_id_type=MESH)
        return carry

    lax.fori_loop(1, shards, greet, 0)
    for device in ({"c": 1 - c}, {"y": 1 - y}, {"y": 1 - y, "c": 1 - c}):
        pl.semaphore_signal(barrier, inc=1, device_id=device, device_id_type=MESH)
    pl.semaphore_wait(barrier, shards + 2)


def rope_tables():
    steps_half = np.arange(ROT // 2, dtype=np.float32)
    inverse = np.float32(1.0) / np.float32(10000.0) ** (steps_half * np.float32(2.0 / ROT))
    turned = np.arange(LENGTH, dtype=np.float32)[:, None] * inverse[None, :].astype(np.float32)
    cosine, sine = (np.float32(part(turned.astype(np.float64))) for part in (np.cos, np.sin))
    none = np.zeros_like(sine)
    rest = np.zeros((LENGTH, HEAD - ROT), np.float32)
    keep = np.concatenate([cosine, cosine, rest + 1], axis=1)
    ahead = np.concatenate([-sine, none, rest], axis=1)
    behind = np.concatenate([none, sine, rest], axis=1)
    return np.stack([np.tile(table, (1, 2)).astype(np.float32) for table in (keep, ahead, behind)])


def gather_events(lines, steps):
    events = []
    for step in range(1, steps):
        for line in lines:
            for which in (0, 1):
                events.append(partial(line.turn, step, which))
    return events


def in_lanes(part, height):
    rows, across = part.shape
    if across < 128:
        part = jnp.concatenate([part, jnp.zeros((rows, 128 - across), f32)], axis=1)
    if rows < height:
        part = jnp.concatenate([part, jnp.zeros((height - rows, 128), f32)], axis=0)
    return part


class Sum:
    def __init__(self, steps, total, got, acc, leaving, kept, swapped, swap_sem, send, recv):
        self.steps, self.total, self.got, self.acc = steps, total, got, acc
        self.leaving, self.kept, self.swapped = leaving, kept, swapped
        self.swap_sem, self.send, self.recv = swap_sem, send, recv
        self.rows = leaving.shape[0]
        self.carried = False

    def part(self, owner, which):
        x = here()[1]
        side = 1 - x if which == 0 else x
        owner = jnp.clip(owner, 0, self.steps - 1)
        return span((owner * 2 + side) * self.rows, self.rows)

    def slot(self, step, which, way):
        index = step - 1 if way == 0 else self.steps + 1 - step
        return self.got.at[index, pl.ds(which * self.rows, self.rows)]

    def hop(self, step, which, way, source):
        z = here()[0]
        device = {"z": jnp.clip(z - 1 if way == 0 else z + 1, 0, self.steps - 1)}
        index = (step - 1) * 4 + which * 2 + way
        target = self.slot(step, which, way)
        source = target if source is None else source
        return remote(source, target, self.send.at[index], self.recv.at[index], device)

    def owner(self, step, way):
        z = here()[0]
        return z - step if way == 0 else z + step

    def sends(self, step, way):
        owner = self.owner(step, way)
        return owner >= 0 if way == 0 else owner < self.steps

    def inner(self, way):
        z = here()[0]
        return z < self.steps - 1 if way == 0 else z > 0

    def turn(self, step, which):
        for way in (0, 1):
            rows = self.part(self.owner(step, way), which)
            if step == self.steps - 1:

                @pl.when(self.sends(step, way))
                def _():
                    self.hop(step, which, way, self.total.at[rows]).start()

            else:

                @pl.when(jnp.logical_and(self.sends(step, way), self.inner(way)))
                def _():
                    if not (self.carried and step == self.steps - 2):
                        self.hop(step + 1, which, way, None).wait_recv()
                    here_now = self.slot(step + 1, which, way)
                    here_now[...] = (
                        here_now[...].astype(f32) + self.total[rows, :].astype(f32)
                    ).astype(bf16)
                    self.hop(step, which, way, here_now).start()

                @pl.when(jnp.logical_and(self.sends(step, way), jnp.logical_not(self.inner(way))))
                def _():
                    self.hop(step, which, way, self.total.at[rows]).start()

    def swap(self):
        x = here()[1]
        return remote(
            self.leaving, self.swapped, self.swap_sem.at[0], self.swap_sem.at[1], {"x": 1 - x}
        )

    def final(self, which):
        z = here()[0]
        self.acc[...] = self.total[self.part(z, which), :].astype(f32)
        for way in (0, 1):

            @pl.when(self.inner(way))
            def _():
                self.hop(1, which, way, None).wait_recv()
                self.acc[...] += self.slot(1, which, way)[...].astype(f32)

        if which == 0:
            self.leaving[...] = self.acc[...].astype(bf16)
            self.swap().start()
        elif self.kept is not None:
            self.kept[...] = self.acc[...]

    def begin(self):
        for which in (0, 1):
            self.turn(self.steps - 1, which)

    def events(self):
        out = []
        for step in range(self.steps - 2, 0, -1):
            out += [partial(self.turn, step, which) for which in (0, 1)]
        return out + [partial(self.final, which) for which in (0, 1)]

    def end(self):
        self.swap().wait_recv()
        self.swap().wait_send()
        for step in range(self.steps - 1 - self.carried, 0, -1):
            for which in (0, 1):
                for way in (0, 1):

                    @pl.when(self.sends(step, way))
                    def _():
                        self.hop(step, which, way, None).wait_send()


class FirstHop(Sum):
    def __init__(self, steps, total, got, rows, send, recv):
        self.steps, self.total, self.got, self.rows = steps, total, got, rows
        self.send, self.recv = send, recv

    def slot(self, step, which, way):
        return self.got.at[way, pl.ds(which * self.rows, self.rows)]

    def end(self):
        z = here()[0]
        last = self.steps - 1
        for way, place in ((0, last - 1), (1, 1)):
            for which in (0, 1):

                @pl.when(z == place)
                def _():
                    self.hop(last, which, way, None).wait_recv()

                @pl.when(self.sends(last, way))
                def _():
                    self.hop(last, which, way, None).wait_send()


class SumPair:
    def __init__(self, *members):
        self.members = members

    def begin(self):
        for member in self.members:
            member.begin()

    def events(self):
        def together(parts):
            for part in parts:
                part()

        return [partial(together, parts) for parts in zip(*(m.events() for m in self.members))]

    def end(self):
        for member in self.members:
            member.end()


def merged(*lists):
    keyed = []
    for number, entries in enumerate(lists):
        for index, entry in enumerate(entries):
            keyed.append(((index + 1) / (len(entries) + 1), number, index, entry))
    return [entry[3] for entry in sorted(keyed, key=lambda item: item[:3])]


def work_loop(count, tile, events):
    def body(index, carry):
        tile(index)
        for turn, due in events.items():

            @pl.when(index == turn)
            def _(due=due):
                for event in due:
                    event()

        return carry

    lax.fori_loop(0, count, body, 0)


def one_each(events):
    return {index: [event] for index, event in enumerate(events)}


def dot(a, b, dims):
    return lax.dot_general(a, b, (dims, ((), ())), preferred_element_type=f32)


TILE = 256


def turned(index, model, rows):
    z = here()[0]
    first = (1 - jnp.minimum(z, 1)) * ((model - 2 * rows) // TILE)
    return lax.rem(index + first, model // TILE)


def tile_of(index):
    return pl.ds(pl.multiple_of(index * TILE, TILE), TILE)


def front_kernel(
    steps,
    small_sizes,
    norm_ref,
    qkv_bias_ref,
    up_own_ref,
    inputs_hbm,
    cot_ref,
    tables_hbm,
    qkv_hbm,
    dense_hbm,
    up_hbm,
    down_hbm,
    vectors_ref,
    attn_out,
    grad_out,
    normed_out,
    cot_out,
    qkv_out,
    dense_out,
    up_out,
    down_full,
    active_out,
    slope_out,
    down_part,
    carry,
    qkv_kept,
    qkv_swapped,
    dense_kept,
    dense_swapped,
    small_ref,
    small_all,
    normed_all,
    cot_all,
    qkv_full,
    dense_full,
    up_full,
    active,
    slope,
    normed,
    qkv_ref,
    dense_ref,
    wide_ref,
    bias_ref,
    bias_up_ref,
    packed_ref,
    g_ref,
    dk_ref,
    dv_ref,
    qkv_got,
    dense_got,
    tables,
    token_send,
    token_recv,
    small_send,
    small_recv,
    swap_sem,
    line_send,
    line_recv,
    sum_swap,
    sum_send,
    sum_recv,
    local,
    load,
    store,
    slope_store,
):
    seq, pair = pl.program_id(0), pl.program_id(1)
    turn_now = seq * pl.num_programs(1) + pair
    z, x, y, c = here()
    shards = steps * 2
    me = z * 2 + x
    depth, width = dense_ref.shape[1:]
    wide = 3 * width
    tokens, model = normed_all.shape
    hidden = up_full.shape[1]
    up_line, qkv_line, dense_line, down_line = (
        Line(
            steps,
            halves,
            full,
            swap_sem.at[index],
            line_send.at[index],
            line_recv.at[index],
            local.at[index],
        )
        for index, (halves, full) in enumerate(
            (
                (wide_ref.at[0], up_full),
                (qkv_ref, qkv_full),
                (dense_ref, dense_full),
                (wide_ref.at[1], down_full),
            )
        )
    )
    lines = [qkv_line, dense_line]
    cots = Tokens(cot_ref, cot_all, token_send.at[0], token_recv.at[0], local.at[4])
    units = Tokens(normed, normed_all, token_send.at[1], token_recv.at[1], local.at[5])
    cuts = (slice(0, wide), slice(wide, wide + width))
    qkv_sum, dense_sum = (
        Sum(
            steps,
            terms,
            got,
            slope.at[0, pl.ds(0, depth), cut],
            wide_ref.at[0, 0, :, cut],
            None,
            swapped,
            sum_swap.at[index],
            sum_send.at[index],
            sum_recv.at[index],
        )
        for index, (terms, got, cut, swapped) in enumerate(
            (
                (qkv_full, qkv_got, cuts[0], qkv_swapped),
                (dense_full, dense_got, cuts[1], dense_swapped),
            )
        )
    )
    narrow = SumPair(qkv_sum, dense_sum)
    first_hop = FirstHop(steps, up_full, carry, depth, sum_send.at[2], sum_recv.at[2])

    def copy_in(index, source, target):
        return pltpu.make_async_copy(source, target, load.at[index])

    narrow_loads = [
        copy_in(kind, qkv_hbm.at[kind], packed_ref.at[pl.ds(kind * depth, depth), 0 : 2 * width])
        for kind in range(3)
    ]
    narrow_loads.append(
        copy_in(3, dense_hbm, packed_ref.at[pl.ds(3 * depth, depth), 0 : 2 * width])
    )

    def wide_loads(index, source):
        return [
            copy_in(
                4 + index * 2 + half,
                source.at[:, half * hidden : (half + 1) * hidden],
                slope.at[half, pl.ds(0, depth)],
            )
            for half in (0, 1)
        ]

    up_loads, down_loads = wide_loads(0, up_hbm), wide_loads(1, down_hbm)

    def copy_out(index, source, target):
        return pltpu.make_async_copy(source, target, store.at[index])

    stores = {
        "cot": copy_out(0, cot_all, cot_out),
        "normed": copy_out(1, normed_all, normed_out),
        "up": copy_out(2, up_full, up_out),
        "active": copy_out(3, active, active_out),
        "qkv": copy_out(4, qkv_full, qkv_out),
        "dense": copy_out(5, dense_full, dense_out),
        "grad": copy_out(6, active.at[:, 0:wide], grad_out),
        "attn": copy_out(7, active.at[:, wide : wide + width], attn_out),
        "down_part": copy_out(8, up_full, down_part),
        "qkv_kept": copy_out(9, slope.at[0, pl.ds(0, depth), cuts[0]], qkv_kept),
        "dense_kept": copy_out(10, slope.at[0, pl.ds(0, depth), cuts[1]], dense_kept),
    }

    def peer(k):
        other = lax.rem(me + k, shards)
        return other, {"z": other // 2, "x": lax.rem(other, 2)}

    def small_copy(k, arrives=False):
        other, device = peer(k)
        slot = other if arrives else me
        return remote(
            small_ref,
            small_all.at[slot],
            small_send.at[k],
            small_recv.at[slot],
            device,
        )

    def each_peer(act):
        def body(k, carry):
            act(k)
            return carry

        lax.fori_loop(1, shards, body, 0)

    def piece(shard, row, size):
        block = small_all[shard].astype(f32)
        across = min(128, size)
        return [block[row + k : row + k + 1, :across] for k in range(size // across)]

    def lower_wide(index, loads):
        for copy in loads:
            copy.wait()
        for half in (0, 1):
            wide_ref[index, half] = slope[half, :depth, :].astype(bf16)

    def gather_all():
        own_loads = [copy_in(8, inputs_hbm, normed), copy_in(9, tables_hbm, tables)]
        for copy in up_loads + narrow_loads + own_loads:
            copy.start()
        barrier = pltpu.get_barrier_semaphore()
        each_peer(
            lambda k: pl.semaphore_signal(
                barrier, inc=1, device_id=peer(k)[1], device_id_type=MESH
            )
        )
        for device in ({"y": 1 - y}, {"c": 1 - c}):
            pl.semaphore_signal(barrier, inc=1, device_id=device, device_id_type=MESH)
        lines_norm = [
            norm_ref[row : row + 1, cut * small_sizes.across : (cut + 1) * small_sizes.across]
            for row in range(4)
            for cut in range(small_sizes.norm_lines)
        ]
        parts = [in_lanes(jnp.concatenate(lines_norm, axis=0), 8)]
        parts += [in_lanes(qkv_bias_ref[...], 3), in_lanes(up_own_ref[...], 5)]
        small_ref[...] = jnp.concatenate(parts, axis=0).astype(bf16)
        for copy in narrow_loads:
            copy.wait()
        for half in (0, 1):
            cut = slice(half * width, (half + 1) * width)
            for kind in range(3):
                at = slice(kind * width, (kind + 1) * width)
                rows = slice(kind * depth, (kind + 1) * depth)
                qkv_ref[half, :, at] = packed_ref[rows, cut].astype(bf16)
            dense_ref[half] = packed_ref[3 * depth : 4 * depth, cut].astype(bf16)
        pl.semaphore_wait(barrier, shards + 1)
        for line in lines:
            line.begin()
        each_peer(lambda k: small_copy(k).start())
        small_all[me] = small_ref[...]
        cots.begin()
        each_peer(lambda k: small_copy(k, arrives=True).wait_recv())
        for row in range(4):
            parts = []
            for shard in range(shards):
                parts += piece(shard, row * small_sizes.norm_lines, small_sizes.norm)
            vectors_ref[row : row + 1, :] = jnp.concatenate(parts, axis=1)
        gain, shift = vectors_ref[0:1, :], vectors_ref[1:2, :]
        chunk = 32

        for copy in own_loads:
            copy.wait()

        def norm(index, carry):
            rows = span(index * chunk, chunk)
            source = normed[rows, :].astype(f32)
            centered = source - jnp.mean(source, axis=1, keepdims=True)
            scale = lax.rsqrt(jnp.mean(centered * centered, axis=1, keepdims=True) + norm_eps)
            normed[rows, :] = (centered * scale * gain + shift).astype(bf16)
            return carry

        lax.fori_loop(0, normed.shape[0] // chunk, norm, 0)
        units.begin()
        for line in lines:
            line.swapped()
        lower_wide(0, up_loads)
        for copy in down_loads:
            copy.start()
        parts = []
        for kind in range(3):
            for part in range(steps):
                parts += piece(x * steps + part, 8 + kind, small_sizes.bias)
        bias_ref[...] = jnp.concatenate(parts, axis=1)
        parts = []
        for part in range(steps):
            parts += piece(x * steps + part, 11, small_sizes.up)
        bias_up_ref[...] = jnp.concatenate(parts, axis=1)
        lower_wide(1, down_loads)
        for step in range(1, steps):
            for line in lines:
                for which in (0, 1):
                    line.turn(step, which)
            if step == max(steps - 2, 1):
                up_line.begin()
                cots.middle()
                units.middle()
        cots.late()
        units.late()
        cots.end()
        units.end()
        for line in lines:
            line.end()
        for name in ("cot", "normed", "qkv", "dense"):
            stores[name].start()
        each_peer(lambda k: small_copy(k).wait_send())
        up_line.swapped()

    def slope_copy(index):
        slot = lax.rem(index, 2)
        return pltpu.make_async_copy(
            slope.at[slot], slope_out.at[tile_of(index), :], slope_store.at[slot]
        )

    def hidden_tile(index):
        at = tile_of(index)
        before = dot(normed_all[at, :], up_full[...], ((1,), (0,))) + bias_up_ref[...]
        inner = (2.0 / 3.141592653589793) ** 0.5
        square = before * before
        bent = jnp.tanh(inner * (before + 0.044715 * (square * before)))
        gate = 0.5 * (1.0 + bent)
        active[at, :] = (before * gate).astype(bf16)

        @pl.when(index >= 2)
        def _():
            slope_copy(index - 2).wait()

        slope[lax.rem(index, 2)] = gate + 0.5 * before * (1.0 - bent * bent) * (
            inner * (1.0 + 3.0 * 0.044715 * square)
        )
        slope_copy(index).start()

    def down_tile(index):
        at = tile_of(index)
        up_full[at, :] = dot(cot_all[:, at], active[...], ((0,), (0,))).astype(bf16)

    up_hops, down_hops = gather_events([up_line], steps), gather_events([down_line], steps)
    sums = narrow.events()

    def up_and_down():
        up_hops[3]()
        down_line.begin()

    when = {(0, 0): up_hops[0], (0, 2): up_hops[1], (1, 2): up_hops[2], (2, 1): up_and_down}

    def check(now, point):
        if (now, point) in when:
            pl.when(turn_now == now)(when[(now, point)])

    def dense_tile(index):
        at = tile_of(index)
        dense_full[at, :] = dot(
            cot_all[:, at], active[:, wide : wide + width], ((0,), (0,))
        ).astype(bf16)

    def qkv_tile(index):
        at = tile_of(turned(index, model, depth))
        qkv_full[at, :] = dot(normed_all[:, at], active[:, :wide], ((0,), (0,))).astype(bf16)

    def finish():
        for name in ("grad", "attn"):
            stores[name].start()
        for name in ("qkv", "dense"):
            stores[name].wait()
        work_loop(model // TILE, dense_tile, {})
        dense_sum.begin()
        work_loop(model // TILE, qkv_tile, {1: [qkv_sum.begin]})
        for event in up_hops[4:]:
            event()
        up_line.end()
        stores["up"].start()
        down_line.swapped()
        for name in ("grad", "attn"):
            stores[name].wait()
        count = tokens // TILE
        work_loop(count, hidden_tile, {2: down_hops[:1], 5: sums[:1]})
        stores["active"].start()
        stores["up"].wait()
        work_loop(model // TILE, down_tile, {1: down_hops[1:2], 4: sums[1:2]})
        stores["down_part"].start()
        slope_copy(count - 2).wait()
        slope_copy(count - 1).wait()
        for event in merged(down_hops[2:-2], sums[2:-2]) + [first_hop.begin] + sums[-2:]:
            event()
        for name in ("qkv_kept", "dense_kept"):
            stores[name].start()
        for event in down_hops[-2:]:
            event()
        down_line.end()
        first_hop.end()
        narrow.end()
        for name in ("cot", "normed", "active", "down_part", "qkv_kept", "dense_kept"):
            stores[name].wait()

    @pl.when(turn_now == 0)
    def _():
        gather_all()

    @pl.when(pair == 0)
    def _():
        def products(index):
            rows, at = tile_of(seq * (LENGTH // TILE) + index), tile_of(index)
            packed_ref[at, :] = dot(normed_all[rows, :], qkv_full[...], ((1,), (0,))) + bias_ref[...]
            g_ref[at, :] = dot(cot_all[rows, :], dense_full[...], ((1,), (0,))).astype(bf16)

        work_loop(LENGTH // TILE, products, {})

    for now in range(4):
        check(now, 0)
    keep, ahead, behind = (tables[index] for index in range(3))
    half = ROT // 2

    def turn(field, sign):
        up = pltpu.roll(field, field.shape[1] - half, 1)
        down = pltpu.roll(field, half, 1)
        return field * keep + sign * (up * ahead + down * behind)

    def lanes_of(kind):
        return pl.ds(pl.multiple_of(kind * width + pair * 2 * HEAD, 2 * HEAD), 2 * HEAD)

    factor = HEAD ** (-0.5)
    query = turn(packed_ref[:, lanes_of(0)], 1.0).astype(bf16) * jnp.asarray(factor, bf16)
    keys = turn(packed_ref[:, lanes_of(1)], 1.0).astype(bf16)
    values = packed_ref[:, lanes_of(2)].astype(bf16)
    grads = g_ref[:, lanes_of(0)]
    inside = lax.broadcasted_iota(jnp.int32, (BLOCK, BLOCK), 1) <= lax.broadcasted_iota(
        jnp.int32, (BLOCK, BLOCK), 0
    )

    mixed_all, dq_all, dk_all, dv_all = [], [], [], []
    for head in range(2):
        lanes = slice(head * HEAD, (head + 1) * HEAD)
        qh, kh, vh, gh = query[:, lanes], keys[:, lanes], values[:, lanes], grads[:, lanes]
        mixed_rows, dq_rows = [], []
        dk_ref[...] = jnp.zeros_like(dk_ref)
        dv_ref[...] = jnp.zeros_like(dv_ref)
        for block in range(LENGTH // BLOCK):
            rows = slice(block * BLOCK, (block + 1) * BLOCK)
            seen = (block + 1) * BLOCK
            q, g, k, v = qh[rows], gh[rows], kh[:seen], vh[:seen]
            scores = dot(q, k, ((1,), (1,)))
            last = jnp.where(inside, scores[:, block * BLOCK :], masked)
            if block > 0:
                scores = jnp.concatenate([scores[:, : block * BLOCK], last], axis=1)
            else:
                scores = last
            top = jnp.max(scores, axis=1, keepdims=True)
            expo = jnp.exp(scores - top)
            probs = expo * (1.0 / jnp.sum(expo, axis=1, keepdims=True))
            low = probs.astype(bf16)
            mixed_rows.append(dot(low, v, ((1,), (0,))))
            grad_probs = dot(g, v, ((1,), (1,)))
            inner = jnp.sum(probs * grad_probs, axis=1, keepdims=True)
            grad_scores = (probs * (grad_probs - inner)).astype(bf16)
            dq_rows.append(dot(grad_scores, k, ((1,), (0,))) * factor)
            dk_ref[:seen] += dot(grad_scores, q, ((0,), (0,)))
            dv_ref[:seen] += dot(low, g, ((0,), (0,)))
        mixed_all.append(jnp.concatenate(mixed_rows, axis=0))
        dq_all.append(jnp.concatenate(dq_rows, axis=0))
        dk_all.append(dk_ref[...])
        dv_all.append(dv_ref[...])
        if head == 0:
            for now in range(4):
                check(now, 1)
    mixed = jnp.concatenate(mixed_all, axis=1)
    gq = turn(jnp.concatenate(dq_all, axis=1), -1.0)
    gk = turn(jnp.concatenate(dk_all, axis=1), -1.0)
    gv = jnp.concatenate(dv_all, axis=1)
    rows = pl.ds(pl.multiple_of(seq * LENGTH, LENGTH), LENGTH)
    for kind, part in enumerate((gq, gk, gv, mixed)):
        active[rows, lanes_of(kind)] = part.astype(bf16)

    for now in range(4):
        check(now, 2)

    pl.when(turn_now == 3)(finish)


def front(norm, qkv_bias, up_bias, inputs, cotangent, tables, qkv, dense, up, down, sizes, steps):
    shards = steps * 2
    rows, model = inputs.shape
    tokens = 8 * rows
    depth, width = dense.shape
    width = width // 2
    wide = 3 * width
    hidden = up.shape[1] // 2
    pairs = width // (2 * HEAD)
    seqs = tokens // LENGTH
    assert seqs * pairs == 4 and wide + width <= hidden and 4 * depth <= LENGTH
    whole = pl.BlockSpec(memory_space=pltpu.VMEM)
    anywhere = pl.BlockSpec(memory_space=pl.ANY)
    dma = pltpu.SemaphoreType.DMA
    hops = max(steps - 1, 1) * 4
    low = {
        name: jax.ShapeDtypeStruct(shape, bf16)
        for name, shape in (
            ("tokens", (tokens, model)),
            ("attn", (tokens, width)),
            ("grad", (tokens, wide)),
            ("hidden", (tokens, hidden)),
            ("qkv", (model, wide)),
            ("dense", (model, width)),
            ("up", (model, hidden)),
        )
    }
    flops = seqs * pairs * 2 * 7 * 2 * LENGTH * LENGTH * HEAD
    flops += 4 * tokens * model * (wide + width + hidden)
    return pl.pallas_call(
        partial(front_kernel, steps, sizes),
        grid=(seqs, pairs),
        in_specs=[whole] * 3 + [anywhere] * 7,
        out_specs=[whole] + [anywhere] * 16,
        out_shape=[
            jax.ShapeDtypeStruct((4, model), f32),
            low["attn"],
            low["grad"],
            low["tokens"],
            low["tokens"],
            low["qkv"],
            low["dense"],
            low["up"],
            low["up"],
            low["hidden"],
            jax.ShapeDtypeStruct((tokens, hidden), f32),
            low["up"],
            jax.ShapeDtypeStruct((2, 2 * depth, hidden), bf16),
            jax.ShapeDtypeStruct((depth, wide), f32),
            jax.ShapeDtypeStruct((depth, wide), bf16),
            jax.ShapeDtypeStruct((depth, width), f32),
            jax.ShapeDtypeStruct((depth, width), bf16),
        ],
        scratch_shapes=[
            pltpu.VMEM((16, 128), bf16),
            pltpu.VMEM((shards, 16, 128), bf16),
            pltpu.VMEM((tokens, model), bf16),
            pltpu.VMEM((tokens, model), bf16),
            pltpu.VMEM((model, wide), bf16),
            pltpu.VMEM((model, width), bf16),
            pltpu.VMEM((model, hidden), bf16),
            pltpu.VMEM((tokens, hidden), bf16),
            pltpu.VMEM((2, TILE, hidden), f32),
            pltpu.VMEM((rows, model), bf16),
            pltpu.VMEM((2, depth, wide), bf16),
            pltpu.VMEM((2, depth, width), bf16),
            pltpu.VMEM((2, 2, depth, hidden), bf16),
            pltpu.VMEM((1, wide), f32),
            pltpu.VMEM((1, hidden), f32),
            pltpu.VMEM((LENGTH, wide), f32),
            pltpu.VMEM((LENGTH, width), bf16),
            pltpu.VMEM((LENGTH, HEAD), f32),
            pltpu.VMEM((LENGTH, HEAD), f32),
            pltpu.VMEM((steps + 1, 2 * depth, wide), bf16),
            pltpu.VMEM((steps + 1, 2 * depth, width), bf16),
            pltpu.VMEM(tables.shape, f32),
            dma((2, 9)),
            dma((2, 9)),
            dma((shards,)),
            dma((shards,)),
            dma((4, 2)),
            dma((4, hops)),
            dma((4, hops)),
            dma((2, 2)),
            dma((3, hops)),
            dma((3, hops)),
            dma((6,)),
            dma((10,)),
            dma((11,)),
            dma((2,)),
        ],
        cost_estimate=pl.CostEstimate(
            flops=flops, bytes_accessed=2**27, transcendentals=seqs * pairs * 2**21
        ),
        compiler_params=pltpu.CompilerParams(
            collective_id=0, has_side_effects=True, vmem_limit_bytes=63 * 2**20
        ),
    )(norm, qkv_bias, up_bias, inputs, cotangent, tables, qkv, dense, up, down)


class TokenSum:
    def __init__(self, product, away, near, one, two, last, out, send, recv):
        self.product, self.away, self.near = product, away, near
        self.one, self.two, self.last, self.out = one, two, last, out
        self.send, self.recv = send, recv
        self.half = out.shape[1] // 2
        self.width = out.shape[2]

    def copy(self, source, target, index, device):
        return remote(source, target, self.send.at[index], self.recv.at[index], device)

    def to_core(self, k):
        c = here()[3]
        return self.copy(self.away.at[k], self.near.at[k], k, {"c": 1 - c})

    def rows(self, which):
        return pl.ds(which * self.half, self.half)

    def first(self, xx, yy):
        x = here()[1]
        source = self.near.at[xx * 2 + yy, self.rows(0)]
        return self.copy(source, self.one.at[yy], 4 + yy, {"x": 1 - x})

    def second(self, xx, yy):
        y = here()[2]
        source = self.near.at[xx * 2 + yy, self.rows(1)]
        return self.copy(source, self.two.at[xx], 6 + xx, {"y": 1 - y})

    def third(self, which):
        _, x, y, _ = here()
        source = self.one.at[1 - y] if which == 0 else self.two.at[1 - x]
        device = {"y": 1 - y} if which == 0 else {"x": 1 - x}
        return self.copy(source, self.last.at[which], 8 + which, device)

    def columns(self):
        size = self.width // 2
        return [slice(index * size, (index + 1) * size) for index in range(4)]

    def give(self, k):
        c = here()[3]
        for cut in self.columns():
            self.away[k, :, cut] = self.product(k * 2 + 1 - c, cut).astype(bf16)
        self.to_core(k).start()

    def take(self, j):
        _, x, y, c = here()
        xx, yy = lax.rem(x + 1 - j // 2, 2), lax.rem(y + 1 - lax.rem(j, 2), 2)
        k = xx * 2 + yy
        self.to_core(k).wait_recv()
        for cut in self.columns():
            term = self.product(k * 2 + c, cut)
            self.near[k, :, cut] = (self.near[k, :, cut].astype(f32) + term).astype(bf16)

        @pl.when(j < 2)
        def _():
            self.first(xx, yy).start()

        @pl.when(lax.rem(j, 2) == 0)
        def _():
            self.second(xx, yy).start()

    def middle(self):
        _, x, y, _ = here()
        self.first(x, 1 - y).wait_recv()
        block = self.one.at[1 - y]
        block[...] = (
            block[...].astype(f32) + self.near[x * 2 + 1 - y, self.rows(0)].astype(f32)
        ).astype(bf16)
        self.third(0).start()
        self.second(1 - x, y).wait_recv()
        block = self.two.at[1 - x]
        block[...] = (
            block[...].astype(f32) + self.near[(1 - x) * 2 + y, self.rows(1)].astype(f32)
        ).astype(bf16)
        self.third(1).start()

    def final(self):
        _, x, y, _ = here()
        self.first(x, y).wait_recv()
        self.second(x, y).wait_recv()
        for which, got in ((0, self.one.at[y]), (1, self.two.at[x])):
            self.third(which).wait_recv()
            for side in (0, 1):
                cut = slice(side * self.width, (side + 1) * self.width)
                self.out[side, self.rows(which), :] = (
                    self.near[x * 2 + y, self.rows(which), cut].astype(f32)
                    + got[:, cut].astype(f32)
                    + self.last[which, :, cut].astype(f32)
                )

    def end_core(self):
        for k in range(4):
            self.to_core(k).wait_send()

    def end(self):
        _, x, y, _ = here()
        for yy in range(2):
            self.first(1 - x, yy).wait_send()
        for xx in range(2):
            self.second(xx, 1 - y).wait_send()
        for which in (0, 1):
            self.third(which).wait_send()


def back_kernel(
    steps,
    small,
    part_hbm,
    carry,
    cot_hbm,
    down_hbm,
    slope_hbm,
    attn_hbm,
    active_hbm,
    dense_hbm,
    normed_hbm,
    grad_packed_hbm,
    qkv_hbm,
    up_hbm,
    inputs_hbm,
    cot_own_hbm,
    vectors_ref,
    down_kept,
    down_swapped,
    up_kept,
    up_swapped,
    output_ref,
    input_grad,
    small_ref,
    rows_all,
    weight,
    slope,
    grad,
    attn,
    active,
    dense,
    away,
    near,
    one,
    two,
    last,
    token_send,
    token_recv,
    free,
    total,
    down_got,
    up_got,
    acc,
    leaving,
    swap_sem,
    sum_send,
    sum_recv,
    load,
    fetch,
    vector_sums,
    small_mine,
    small_got,
    near_got,
    small_send,
    small_recv,
):
    z, x, y, c = here()
    loads = [
        pltpu.make_async_copy(source, target, load.at[index])
        for index, (source, target) in enumerate(
            (
                (part_hbm, total),
                (cot_hbm, rows_all),
                (down_hbm, weight),
                (attn_hbm, attn),
                (active_hbm, active),
                (dense_hbm, dense),
            )
        )
    ]
    for copy in loads[:1] + loads[2:] + loads[1:2]:
        copy.start()
    carried = [
        (z == place, pltpu.make_async_copy(carry.at[way], down_got.at[slot], load.at[8]))
        for way, place, slot in ((0, steps - 2, steps - 2), (1, 1, 2))
    ]
    for here_now, copy in carried:
        pl.when(here_now)(copy.start)
    greet_wide(steps)

    def slope_copy(index):
        slot = lax.rem(index, 2)
        return pltpu.make_async_copy(
            slope_hbm.at[tile_of(index), :], slope.at[slot], fetch.at[slot]
        )

    slope_copy(0).start()
    tokens, model = cot_hbm.shape
    count = tokens // TILE
    down_sum, up_sum = (
        Sum(
            steps,
            terms,
            got,
            acc,
            leaving,
            None,
            swapped,
            swap_sem.at[index],
            sum_send.at[index],
            sum_recv.at[index],
        )
        for index, (terms, got, swapped) in enumerate(
            ((total, down_got, down_swapped), (active, up_got, up_swapped))
        )
    )
    keeps = [
        pltpu.make_async_copy(acc, kept, load.at[index + 6])
        for index, kept in enumerate((down_kept, up_kept))
    ]

    def out_product(tile, cut):
        at = tile_of(tile)
        return dot(attn[at, :], dense[cut, :], ((1,), (1,))) + dot(
            active[at, :], weight[cut, :], ((1,), (1,))
        )

    wide = grad_packed_hbm.shape[1]

    def normed_product(tile, cut):
        at = tile_of(tile)
        return dot(rows_all[at, :wide], rows_all[cut, wide : 2 * wide], ((1,), (1,))) + dot(
            grad[at, :], weight[cut, :], ((1,), (1,))
        )

    buffers = (away, near, one, two, last, slope)
    out_tokens, normed_tokens = (
        TokenSum(product, *buffers, token_send.at[index], token_recv.at[index])
        for index, product in enumerate((out_product, normed_product))
    )
    down_sum.carried = True
    loads[0].wait()
    for here_now, copy in carried:
        pl.when(here_now)(copy.wait)
    events = down_sum.events()
    for event in events[:2]:
        event()
    for copy in loads[2:]:
        copy.wait()
    work_loop(4, out_tokens.give, {})
    work_loop(4, out_tokens.take, {3: events[2:3]})
    out_tokens.end_core()
    inputs_load = pltpu.make_async_copy(inputs_hbm, away.at[0], load.at[0])
    cot_load = pltpu.make_async_copy(cot_own_hbm, away.at[1], load.at[1])
    inputs_load.start()
    loads[1].wait()

    def grad_tile(index, bias_sum):
        at = tile_of(index)

        @pl.when(index + 1 < count)
        def _():
            slope_copy(index + 1).start()

        slope_copy(index).wait()
        term = dot(rows_all[at, :], weight[...], ((1,), (0,))) * slope[lax.rem(index, 2)]
        low = term.astype(bf16)
        grad[at, :] = low

        @pl.when(index == 4)
        def _():
            for event in events[3:-2]:
                event()

        return bias_sum + jnp.sum(low.astype(f32), axis=0, keepdims=True)

    hidden_sum = lax.fori_loop(0, count, grad_tile, jnp.zeros((1, slope.shape[2]), f32))
    normed_load = pltpu.make_async_copy(normed_hbm, rows_all, load.at[1])
    normed_load.start()
    normed_load.wait()

    def up_tile(index):
        at = tile_of(turned(index, model, leaving.shape[0]))
        active[at, :] = dot(rows_all[:, at], grad[...], ((0,), (0,))).astype(bf16)

    work_loop(model // TILE, up_tile, {1: [up_sum.begin]})
    late = [
        pltpu.make_async_copy(grad_packed_hbm, rows_all.at[:, 0:wide], load.at[2]),
        pltpu.make_async_copy(qkv_hbm, rows_all.at[:, wide : 2 * wide], load.at[3]),
        pltpu.make_async_copy(up_hbm, weight, load.at[4]),
    ]
    for copy in late:
        copy.start()
    up_events = up_sum.events()
    out_tokens.middle()
    events[-2]()
    out_tokens.final()
    inputs_load.wait()
    chunk = 32

    def both(ref, rows):
        return jnp.concatenate([ref[0, rows, :], ref[1, rows, :]], axis=1)

    def finish_output(index, carry):
        rows = span(index * chunk, chunk)
        output_ref[rows, :] = (
            away[0, rows, :].astype(f32)
            + both(slope, rows)
            + vectors_ref[2:3, :]
            + vectors_ref[3:4, :]
        ).astype(bf16)
        return carry

    lax.fori_loop(0, output_ref.shape[0] // chunk, finish_output, 0)
    out_tokens.end()
    near_by = ({"x": 1 - x}, {"y": 1 - y}, {"c": 1 - c})
    for index, device in enumerate(near_by):
        pl.semaphore_signal(free.at[index], inc=1, device_id=device, device_id_type=MESH)
    events[-1]()
    keeps[0].start()
    for copy in late:
        copy.wait()
    for index in range(3):
        pl.semaphore_wait(free.at[index], 1)
    work_loop(4, normed_tokens.give, {})
    work_loop(4, normed_tokens.take, {1: up_events[:1], 3: up_events[1:2]})
    normed_tokens.end_core()
    inputs_load.start()
    cot_load.start()
    packed_sum = jnp.zeros((1, wide), f32)

    def packed_tile(index, packed_sum):
        rows = rows_all[tile_of(index), :wide].astype(f32)
        return packed_sum + jnp.sum(rows, axis=0, keepdims=True)

    packed_sum = lax.fori_loop(0, count, packed_tile, packed_sum)
    for event in up_events[2:3]:
        event()
    normed_tokens.middle()
    for event in up_events[3:-2]:
        event()
    normed_tokens.final()
    inputs_load.wait()
    cot_load.wait()
    vector_sums[...] = jnp.zeros_like(vector_sums)
    gain = vectors_ref[0:1, :]

    def norm(index, carry):
        rows = span(index * chunk, chunk)
        source = away[0, rows, :].astype(f32)
        centered = source - jnp.mean(source, axis=1, keepdims=True)
        scale = lax.rsqrt(jnp.mean(centered * centered, axis=1, keepdims=True) + norm_eps)
        unit = centered * scale
        grads = both(slope, rows)
        cot = away[1, rows, :].astype(f32)
        vector_sums[0] += jnp.sum(grads * unit, axis=0, keepdims=True)
        vector_sums[1] += jnp.sum(grads, axis=0, keepdims=True)
        vector_sums[2] += jnp.sum(cot, axis=0, keepdims=True)
        grad_unit = grads * gain
        result = cot + scale * (
            grad_unit
            - jnp.mean(grad_unit, axis=1, keepdims=True)
            - unit * jnp.mean(grad_unit * unit, axis=1, keepdims=True)
        )
        half = result.shape[1] // 2
        slope[0, rows, :] = result[:, :half]
        slope[1, rows, :] = result[:, half:]
        return carry

    lax.fori_loop(0, output_ref.shape[0] // chunk, norm, 0)
    side = slope.shape[2]
    input_out = [
        pltpu.make_async_copy(
            slope.at[index], input_grad.at[:, index * side : (index + 1) * side], load.at[index + 4]
        )
        for index in (0, 1)
    ]
    for copy in input_out:
        copy.start()
    shards = steps * 2
    small_mine[...] = jnp.zeros_like(small_mine)
    vectors = [vector_sums[row] for row in range(3)]
    for shard in range(shards):
        for row in range(3):
            put_lines(
                small_mine, shard, row * small.norm_lines, vectors[row], shard * small.norm, small.norm
            )
    for part in range(steps):
        shard = x * steps + part
        for kind in range(3):
            start = kind * steps * small.bias + part * small.bias
            put_lines(small_mine, shard, 8 + kind, packed_sum, start, small.bias)
        put_lines(small_mine, shard, 11, hidden_sum, part * small.up, small.up)
    small_sums = SmallSum(steps, small_mine, small_ref, small_got, near_got, small_send, small_recv)
    small_sums.begin()
    down_sum.end()
    keeps[0].wait()
    up_events[-2]()
    small_sums.finish()
    up_events[-1]()
    keeps[1].start()
    for copy in input_out:
        copy.wait()
    normed_tokens.end()
    up_sum.end()
    keeps[1].wait()


def back(
    part,
    carry,
    cot,
    down,
    slope,
    attn,
    active,
    dense,
    normed,
    grad_packed,
    qkv,
    up,
    inputs,
    cot_own,
    vectors,
    small,
    steps,
):
    tokens, model = cot.shape
    hidden = down.shape[1]
    rows = tokens // 8
    depth = model // (2 * steps)
    shards = 2 * steps
    got = max(steps - 1, 1)
    anywhere = pl.BlockSpec(memory_space=pl.ANY)
    whole = pl.BlockSpec(memory_space=pltpu.VMEM)
    dma = pltpu.SemaphoreType.DMA
    half = pltpu.VMEM((2, rows // 2, model), bf16)
    return pl.pallas_call(
        partial(back_kernel, steps, small),
        in_specs=[anywhere] * 14 + [whole],
        out_specs=[anywhere] * 4 + [whole, anywhere, whole],
        out_shape=[
            jax.ShapeDtypeStruct((depth, hidden), f32),
            jax.ShapeDtypeStruct((depth, hidden), bf16),
            jax.ShapeDtypeStruct((depth, hidden), f32),
            jax.ShapeDtypeStruct((depth, hidden), bf16),
            jax.ShapeDtypeStruct((rows, model), bf16),
            jax.ShapeDtypeStruct((rows, model), f32),
            jax.ShapeDtypeStruct((16, 128), f32),
        ],
        scratch_shapes=[
            pltpu.VMEM((tokens, model), bf16),
            pltpu.VMEM((model, hidden), bf16),
            pltpu.VMEM((2, TILE, hidden), f32),
            pltpu.VMEM((tokens, hidden), bf16),
            pltpu.VMEM(attn.shape, bf16),
            pltpu.VMEM((tokens, hidden), bf16),
            pltpu.VMEM(dense.shape, bf16),
            pltpu.VMEM((4, rows, model), bf16),
            pltpu.VMEM((4, rows, model), bf16),
            half,
            half,
            half,
            dma((2, 10)),
            dma((2, 10)),
            pltpu.SemaphoreType.REGULAR((3,)),
            pltpu.VMEM((model, hidden), bf16),
            pltpu.VMEM((steps + 1, 2 * depth, hidden), bf16),
            pltpu.VMEM((steps + 1, 2 * depth, hidden), bf16),
            pltpu.VMEM((depth, hidden), f32),
            pltpu.VMEM((depth, hidden), bf16),
            dma((2, 2)),
            dma((2, got * 4)),
            dma((2, got * 4)),
            dma((9,)),
            dma((2,)),
            pltpu.VMEM((3, 1, model), f32),
            pltpu.VMEM((shards, 16, 128), f32),
            pltpu.VMEM((shards, 16, 128), f32),
            pltpu.VMEM((4, 8, 128), f32),
            dma((shards + 3,)),
            dma((shards + 3,)),
        ],
        cost_estimate=pl.CostEstimate(flops=5 * 10**10, bytes_accessed=2**27, transcendentals=0),
        compiler_params=pltpu.CompilerParams(
            collective_id=4, has_side_effects=True, vmem_limit_bytes=60 * 2**20
        ),
    )(
        part,
        carry,
        cot,
        down,
        slope,
        attn,
        active,
        dense,
        normed,
        grad_packed,
        qkv,
        up,
        inputs,
        cot_own,
        vectors,
    )


def adam(weight, grad, first, second, rate, decay):
    first_new = beta_one * first + (1.0 - beta_one) * grad
    second_new = beta_two * second + (1.0 - beta_two) * grad * grad
    scaled_first = first_new * (1.0 / (1.0 - beta_one**STEP))
    scaled_second = second_new * (1.0 / (1.0 - beta_two**STEP))
    weight_new = weight - rate * (
        scaled_first / (jnp.sqrt(scaled_second) + epsilon) + decay * weight
    )
    return (grad, weight_new, first_new, second_new)


def update_kernel(sizes, *refs):
    x = lax.axis_index("x")
    ins, outs = list(refs[:32]), list(refs[32:])
    for source, target in zip(ins[:2], outs[:2]):
        target[...] = source[...]
    ins, outs = ins[2:], outs[2:]

    def halves(kept, swapped):
        kept, swapped = kept, swapped.astype(f32)
        left = jnp.where(x == 0, kept, swapped)
        return left, jnp.where(x == 0, swapped, kept)

    def put(at, grad, rate, decay, index=()):
        weight, first, second = (ref[index] if index else ref[...] for ref in ins[at : at + 3])
        for ref, value in zip(outs, adam(weight, grad, first, second, rate, decay)):
            if index:
                ref[index] = value
            else:
                ref[...] = value

    kept, swapped = ins[0], ins[1]
    width = kept.shape[1] // 3
    for kind in range(3):
        cut = slice(kind * width, (kind + 1) * width)
        for side, grad in enumerate(halves(kept[:, cut], swapped[:, cut])):
            at = (kind, slice(None), slice(side * width, (side + 1) * width))
            put(2, grad, 0.02, 0.1, at)
    ins, outs = ins[5:], outs[4:]
    for _ in range(3):
        kept, swapped = ins[0], ins[1]
        width = kept.shape[1]
        for side, grad in enumerate(halves(kept[...], swapped[...])):
            put(2, grad, 0.02, 0.1, (slice(None), slice(side * width, (side + 1) * width)))
        ins, outs = ins[5:], outs[4:]

    @pl.when(pl.program_id(0) == 0)
    def _():
        nonlocal ins, outs
        small = ins[0][...]
        ins = ins[1:]
        put(0, small[8:11, : sizes.bias], 0.2, 0.0)
        ins, outs = ins[3:], outs[4:]
        across = min(128, sizes.up)
        put(0, small[11 : 11 + sizes.up // across, :across], 0.2, 0.0)
        ins, outs = ins[3:], outs[4:]
        lines = sizes.norm_lines
        rows = []
        for row in (0, 1, 2, 2):
            cuts = [small[row * lines + k : row * lines + k + 1, : sizes.across] for k in range(lines)]
            rows.append(jnp.concatenate(cuts, axis=1))
        put(0, jnp.concatenate(rows, axis=0), 0.2, 0.0)


def update(final, large, small, sizes):
    depth = large[0][0].shape[0]
    height = min(64, depth)

    def spec(part):
        if part.ndim == 3:
            return pl.BlockSpec((3, height, part.shape[2]), lambda i: (0, i, 0))
        return pl.BlockSpec((height, part.shape[1]), lambda i: (i, 0))

    def fixed(part):
        return pl.BlockSpec(part.shape, lambda i: (0, 0))

    def share(part):
        return pl.BlockSpec((part.shape[0] * height // depth, part.shape[1]), lambda i: (i, 0))

    args = [*final, *(part for group in large for part in group), small[0]]
    in_specs = [share(part) for part in final]
    in_specs += [spec(part) for part in args[2:-1]] + [fixed(small[0])]
    out_specs = [share(part) for part in final]
    out_shape = [jax.ShapeDtypeStruct(part.shape, part.dtype) for part in final]
    for group in large:
        out_specs += [spec(group[2])] * 4
        out_shape += [jax.ShapeDtypeStruct(group[2].shape, f32)] * 4
    for group in small[1:]:
        args += list(group)
        in_specs += [fixed(part) for part in group]
        out_specs += [fixed(group[0])] * 4
        out_shape += [jax.ShapeDtypeStruct(group[0].shape, f32)] * 4
    return pl.pallas_call(
        partial(update_kernel, sizes),
        grid=(depth // height,),
        in_specs=in_specs,
        out_specs=out_specs,
        out_shape=out_shape,
        cost_estimate=pl.CostEstimate(flops=3 * 10**7, bytes_accessed=5 * 10**7, transcendentals=0),
        compiler_params=pltpu.CompilerParams(vmem_limit_bytes=60 * 2**20),
    )(*args)


def on_device(
    inputs,
    cotangent,
    qkv_weight,
    qkv_first,
    qkv_second,
    dense_weight,
    dense_first,
    dense_second,
    up_weight,
    up_first,
    up_second,
    down_weight,
    down_first,
    down_second,
    qkv_bias,
    qkv_bias_first,
    qkv_bias_second,
    up_bias,
    up_bias_first,
    up_bias_second,
    norm_vectors,
    norm_first,
    norm_second,
):
    steps = lax.axis_size("z")
    shards = steps * lax.axis_size("x")
    z, x, y, c = (lax.axis_index(name) for name in ("z", "x", "y", "c"))
    rows, model = inputs.shape
    depth = qkv_weight.shape[0]
    own_bias = qkv_bias.shape[1]
    own_up = up_bias.shape[0]
    own_norm = norm_vectors.shape[1]

    sizes = SmallSizes(own_norm, own_bias, own_up)

    def in_rows(part):
        return part.reshape(-1, min(128, own_up))

    kinds_first = (1, 0, 2)
    qkv_parts = [part.transpose(kinds_first) for part in (qkv_weight, qkv_first, qkv_second)]
    (
        vectors,
        attn,
        grad_packed,
        normed_all,
        grad_all,
        qkv_full,
        dense_full,
        up_full,
        down_full,
        active,
        slope,
        down_part,
        carry,
        qkv_kept,
        qkv_swapped,
        dense_kept,
        dense_swapped,
    ) = front(
        norm_vectors,
        qkv_bias,
        in_rows(up_bias),
        inputs,
        cotangent,
        rope_tables(),
        qkv_parts[0],
        dense_weight,
        up_weight,
        down_weight,
        sizes,
        steps,
    )
    (
        down_kept,
        down_swapped,
        up_kept,
        up_swapped,
        output,
        input_grad,
        small_sums,
    ) = back(
        down_part,
        carry,
        grad_all,
        down_full,
        slope,
        attn,
        active,
        dense_full,
        normed_all,
        grad_packed,
        qkv_full,
        up_full,
        inputs,
        cotangent,
        vectors,
        sizes,
        steps,
    )

    large = (
        (qkv_kept, qkv_swapped, *qkv_parts),
        (dense_kept, dense_swapped, dense_weight, dense_first, dense_second),
        (up_kept, up_swapped, up_weight, up_first, up_second),
        (down_kept, down_swapped, down_weight, down_first, down_second),
    )
    little = (
        small_sums,
        (qkv_bias, qkv_bias_first, qkv_bias_second),
        tuple(in_rows(part) for part in (up_bias, up_bias_first, up_bias_second)),
        (norm_vectors, norm_first, norm_second),
    )
    new = list(update((output, input_grad), large, little, sizes))
    new[2:6] = [part.transpose(kinds_first) for part in new[2:6]]
    new[22:26] = [part.reshape(-1) for part in new[22:26]]
    return tuple(new)


def solution(mesh):
    data, tensor = mesh.shape["dp"], mesh.shape["tensor"]
    fine = Mesh(mesh.devices.reshape(data // 2, 2, tensor // 2, 2), ("z", "x", "y", "c"))
    dp, tp = ("z", "x"), ("y", "c")
    tokens = P(dp + tp, None)
    cube = P(dp, None, tp)
    matrix = P(dp, tp)
    bias_wide, bias, norm = P(None, tp + dp), P(tp + dp), P(None, dp)
    in_specs = (
        (tokens,) * 2
        + (cube,) * 3
        + (matrix,) * 9
        + (bias_wide,) * 3
        + (bias,) * 3
        + (norm,) * 3
    )
    out_specs = (
        (tokens,) * 2
        + (cube,) * 4
        + (matrix,) * 12
        + (bias_wide,) * 4
        + (bias,) * 4
        + (norm,) * 4
    )
    return jax.shard_map(
        on_device, mesh=fine, in_specs=in_specs, out_specs=out_specs, check_vma=False
    )
```

time: 1760 us -> 413 us (0.23)
  waiting for transfers between devices: 1210 us -> 0 us
  Pallas kernels: 0 us -> 411 us
  matrix products: 246 us -> 0 us
  blocking collectives: 104 us -> 0 us
  other arithmetic: 85.5 us -> 0 us
  local copies, waits for them, and re-layouts: 75.8 us -> 0 us
    reduce_scatter x6 -> x0, waiting for transfers between devices: 872 us -> none  [the longest x1 279 us: on_device(): lax.psum_scatter(up_rows, 'dp', scatter_dimension=0, tiled=True)]
    pallas_call x0 -> x3, Pallas kernels: none -> 411 us  [the longest x1 255 us: front(): pl.pallas_call(partial(front_kernel, steps, sizes), grid=(seqs, pairs), i...]
    all_gather x6 -> x0, waiting for transfers between devices: 255 us -> none  [the longest x1 128 us: on_device(): lax.all_gather(lowered[2], 'dp', axis=0, tiled=True)]
    dot_general x26 -> x0, matrix products: 246 us -> none  [the longest x4 36.6 us: score_block(): jnp.einsum('bhe,lhe->hbl', part, keys, preferred_element_type=jnp.float32)]
    unnamed x16 -> x0, waiting for transfers between devices: 81.9 us -> none
    all_gather x3 -> x0, blocking collectives: 78.8 us -> none  [the longest x1 32 us: on_device(): lax.all_gather(lowered[4], 'dp', axis=1, tiled=True)]
    dynamic_update_slice x6 -> x0, local copies, waits for them, and re-layouts: 43.4 us -> none  [the longest x4 43.4 us: attend_back(): lax.scan(one_block, (zeros, zeros), (starts, top, total))]
    convert_element_type x10 -> x0, other arithmetic: 28.2 us -> none  [the longest x2 23 us: one_block(): grad_scores = (probs * (grad_probs - inner)).astype(jnp.bfloat16)]
  transfers between devices with their start and end apart: 14 -> 0, of which waited for: 12 -> 0; matrix products, arithmetic and copies ran while one was open for 19% -> 0% of each run, Pallas kernels for 0% -> 0%
where the time goes in v1:
time: 413 us; the launch traced here: 412 us
  Pallas kernels  411 us (100%)
    pallas_call x1, Pallas kernels, front(): pl.pallas_call(partial(front_kernel, steps, sizes), grid=(seqs, pairs), i...  255 us
    pallas_call x1, Pallas kernels, back(): pl.pallas_call(partial(back_kernel, steps, small), in_specs=[anywhere] *...  137 us
    pallas_call x1, Pallas kernels, update(): pl.pallas_call(partial(update_kernel, sizes), grid=(depth // height,), in...  19.3 us

profile of v1, /device:TPU:0, one launch (start us, length us, event | category | flops | bytes accessed | tf_op | source)
XLA Modules:
  0.0 412.3 jit_solution(365665456986073126)
XLA Ops:
  0.7 255.1 %shard_map.463 = (f32[4,2048]{1,0:T(4,128)}, bf16[2048,256]{1,0:T(8,128)(2,1)}, bf16[2048,768]{1,0:T(8,128)(2,1)}, bf16[2048,2048]{1,0:T(8,128)(2,1)}, bf16[2048...) custom-call(f32[4,256]{1,0:T(4,128)} %refs_29_.1, ...), custom_call_target="tpu_custom_call" | custom-call | flops 41875931136 | bytes 134217728 | tf_op jit(solution)/shard_map/pallas_call | solution.py:997
  255.8 137.0 %shard_map.464 = (f32[256,1024]{1,0:T(8,128)}, bf16[256,1024]{1,0:T(8,128)(2,1)}, f32[256,1024]{1,0:T(8,128)}, bf16[256,1024]{1,0:T(8,128)(2,1)}, bf16[256,2048]...) custom-call(bf16[2048,1024]{1,0:T(8,128)(2,1)} %get-tuple-element.84.part_hbm, ...), custom_call_target="tpu_custom_call" | custom-call | flops 49999998976 | bytes 134217728 | tf_op jit(solution)/shard_map/pallas_call | solution.py:1500
  392.8 19.3 %shard_map.465 = (bf16[256,2048]{1,0:T(8,128)(2,1)}, f32[256,2048]{1,0:T(8,128)}, f32[3,256,512]{2,1,0:T(8,128)}, f32[3,256,512]{2,1,0:T(8,128)}, f32[3,256,512]...) custom-call(bf16[256,2048]{1,0:T(8,128)(2,1)} %get-tuple-element.97., ...), custom_call_target="tpu_custom_call" | custom-call | flops 30000000 | bytes 50000000 | tf_op jit(solution)/shard_map/pallas_call | solution.py:1661
